TPU v7x, 128 devices: a whole 4x4x4 slice. The times are simulated.
128 devices in a mesh: pp: 8 (over y, x_lo), ep: 16 (over x_hi, z, core).
Axes of the slice: x: 4 (x_hi: 2, x_lo: 2; x = x_hi * 2 + x_lo), y: 4, z: 4, core: 2. Of those that a mesh axis runs over, the one named last changes fastest.
Arguments:
- fwd_sent: bfloat16 [8, 2048, 7168], P('pp', 'ep'), may hold values from -40 to 40
- bwd_sent: bfloat16 [8, 2048, 7168], P('pp', 'ep'), may hold values from -12 to 12
- bwd_saved: bfloat16 [8, 2048, 7168], P('pp', 'ep'), may hold values from -40 to 40
- bwd_pre: bfloat16 [8, 2048, 2, 2048], P('pp', 'ep'), may hold values from -5 to 5
- fwd_route: int32 [8, 2048, 2], P('pp', 'ep'), may hold values from 0 to 3, all different within a row; in each aligned block of 128 rows (0 to 127, 128 to 255, ..., all dimensions but the last counted through in order) at most 72 rows name the same one
- bwd_route: int32 [8, 2048, 2], P('pp', 'ep'), may hold values from 0 to 3, all different within a row; in each aligned block of 128 rows (0 to 127, 128 to 255, ..., all dimensions but the last counted through in order) at most 72 rows name the same one
- fwd_gate: float32 [8, 2048, 2], P('pp', 'ep'), may hold values from 0.2 to 1
- bwd_gate: float32 [8, 2048, 2], P('pp', 'ep'), may hold values from 0.2 to 1
- gain: float32 [8, 7168], P('pp'), may hold values from 0.5 to 1.5
- w_in: bfloat16 [8, 28672, 2048], P('pp', 'ep'), may hold values from -0.0625 to 0.0625
- w_out: bfloat16 [8, 1024, 28672], P('pp', None, 'ep'), may hold values from -0.1875 to 0.1875
Outputs:
- fwd_out: bfloat16 [8, 2048, 7168], P('pp', 'ep')
- bwd_out: bfloat16 [8, 2048, 7168], P('pp', 'ep')
- gain_grad: float32 [8, 7168], P('pp')
Inputs may be any that keep to these rules, and one draw needn't show every extreme that they name: `fwd_route`: each token's 2 ids differ. In the 128 rows of one device no expert is named more than 72 times, and in every draw some expert is named exactly 72 times by the rows of some device. `bwd_route`: as for fwd_route.
All inputs are finite; a program needn't handle non-finite values.
Results may differ from a plain program's by a relative error of at most 0.0071.
Values may be sent and summed in bfloat16 or wider, within the bound.
A program may use at most 192 MiB of HBM per device.

v0:
```python
import jax
import jax.numpy as jnp
from jax import lax
from jax.sharding import PartitionSpec as P

FF = 1024
EXPERTS = 4
TOP = 2
CAP = 72


epsilon = 1e-06


def shifted(block, axis, distance):
    devices = range(lax.axis_size(axis))
    route = [((i - distance) % len(devices), i) for i in devices]
    return lax.ppermute(block, axis, route)


def partner_2(value, axis, stride):
    mask = 2**stride
    pairs = [(source, source ^ mask) for source in range(lax.axis_size(axis))]
    return lax.ppermute(value, axis, pairs)


def slot_place(route_flat, expert_total, capacity):
    expert_ids = jnp.arange(expert_total, dtype=jnp.int32)
    one_hot = (route_flat[..., None] == expert_ids).astype(jnp.int32)
    earlier = jnp.cumsum(one_hot, axis=-2) - one_hot
    return route_flat * capacity + jnp.sum(earlier * one_hot, axis=-1)


def on_device(
    fwd_sent,
    bwd_sent,
    bwd_saved,
    bwd_pre,
    fwd_route,
    bwd_route,
    fwd_gate,
    bwd_gate,
    gain,
    w_in,
    w_out,
):
    arrived = shifted(fwd_sent, "pp", 1)[0]
    returned = shifted(bwd_sent, "pp", -1)[0]
    groups = lax.axis_size("ep")
    slices = groups // EXPERTS
    bit_count = slices.bit_length() - 1
    tokens_here, feature_count = arrived.shape
    piece_width = feature_count // slices
    pair_count = tokens_here * TOP
    gain_row = gain[0]
    weight_in = w_in[0]
    weight_out = w_out[0]
    contract = (((1,), (1,)), ((), ()))

    def outbound(pair_rows, place):
        inverse = (
            jnp.full((EXPERTS * CAP,), pair_count, jnp.int32)
            .at[place]
            .set(jnp.arange(pair_count, dtype=jnp.int32))
        )
        padded = jnp.concatenate(
            [pair_rows, jnp.zeros((1, pair_rows.shape[1]), pair_rows.dtype)], axis=0
        )
        return padded[inverse]

    def split_send(rows):
        return (
            rows.reshape(EXPERTS, CAP, slices, piece_width)
            .transpose(0, 2, 1, 3)
            .reshape(groups, CAP, piece_width)
        )

    def join_back(received):
        return (
            received.reshape(EXPERTS, slices, CAP, piece_width)
            .transpose(0, 2, 1, 3)
            .reshape(EXPERTS * CAP, feature_count)
        )

    values = arrived.astype(jnp.float32)
    inv_rms = lax.rsqrt(jnp.mean(values * values, axis=-1, keepdims=True) + epsilon)
    normed = (values * inv_rms * gain_row).astype(jnp.bfloat16)
    place_fwd = slot_place(fwd_route[0].reshape(-1), EXPERTS, CAP)
    send_rows = split_send(outbound(jnp.repeat(normed, TOP, axis=0), place_fwd))
    saved_values = bwd_saved[0].astype(jnp.float32)
    saved_inv = lax.rsqrt(jnp.mean(saved_values * saved_values, axis=-1, keepdims=True) + epsilon)
    grad_values = returned.astype(jnp.float32)
    weighted = (
        (bwd_gate[0][:, :, None] * grad_values[:, None, :])
        .astype(jnp.bfloat16)
        .reshape(pair_count, feature_count)
    )
    place_bwd = slot_place(bwd_route[0].reshape(-1), EXPERTS, CAP)
    send_grad = split_send(outbound(weighted, place_bwd))
    pre_out = outbound(bwd_pre[0].reshape(pair_count, 2 * FF), place_bwd)
    row_width = pre_out.shape[1]
    spread = jnp.broadcast_to(
        pre_out.reshape(EXPERTS, 1, CAP, row_width), (EXPERTS, slices, CAP, row_width)
    )
    send_pre = spread.reshape(groups, CAP, row_width)
    recv_rows = lax.all_to_all(send_rows, "ep", split_axis=0, concat_axis=0, tiled=True)
    current = lax.optimization_barrier(
        jnp.dot(
            recv_rows.reshape(-1, piece_width), weight_in, preferred_element_type=jnp.float32
        ).astype(jnp.bfloat16)
    )
    fwd_sum = current.astype(jnp.float32)
    for bit_index in range(bit_count):
        partner = partner_2(current, "ep", bit_index)
        fwd_sum = current.astype(jnp.float32) + partner.astype(jnp.float32)
        if bit_index + 1 < bit_count:
            current = lax.optimization_barrier(fwd_sum.astype(jnp.bfloat16))
    pre_three = fwd_sum.reshape(-1, 2, FF)
    result = jnp.dot(
        (jax.nn.silu(pre_three[:, 0]) * pre_three[:, 1]).astype(jnp.bfloat16),
        weight_out,
        preferred_element_type=jnp.float32,
    ).astype(jnp.bfloat16)
    result_fwd = result.reshape(groups, CAP, piece_width)
    back_out = lax.all_to_all(result_fwd, "ep", split_axis=0, concat_axis=0, tiled=True)
    recv_grad, recv_pre = (
        lax.all_to_all(send_grad, "ep", split_axis=0, concat_axis=0, tiled=True),
        lax.all_to_all(send_pre, "ep", split_axis=0, concat_axis=0, tiled=True),
    )
    current = lax.optimization_barrier(
        lax.dot_general(
            recv_grad.reshape(-1, piece_width),
            weight_out,
            contract,
            preferred_element_type=jnp.float32,
        ).astype(jnp.bfloat16)
    )
    bwd_sum = current.astype(jnp.float32)
    for bit_index in range(bit_count):
        partner = partner_2(current, "ep", bit_index)
        bwd_sum = current.astype(jnp.float32) + partner.astype(jnp.float32)
        if bit_index + 1 < bit_count:
            current = lax.optimization_barrier(bwd_sum.astype(jnp.bfloat16))
    pre_vals = recv_pre.reshape(-1, 2, FF).astype(jnp.float32)
    gate_pre = pre_vals[:, 0]
    up_pre = pre_vals[:, 1]
    sigma = jax.nn.sigmoid(gate_pre)
    slope = sigma * (1.0 + gate_pre * (1.0 - sigma))
    result = lax.dot_general(
        jnp.stack([bwd_sum * up_pre * slope, bwd_sum * gate_pre * sigma], axis=1)
        .astype(jnp.bfloat16)
        .reshape(-1, 2 * FF),
        weight_in,
        contract,
        preferred_element_type=jnp.float32,
    ).astype(jnp.bfloat16)
    result_bwd = result.reshape(groups, CAP, piece_width)
    back_grad = lax.all_to_all(result_bwd, "ep", split_axis=0, concat_axis=0, tiled=True)
    pair_out = join_back(back_out)[place_fwd].reshape(tokens_here, TOP, feature_count)
    fwd_out = (
        values + jnp.sum(fwd_gate[0][:, :, None] * pair_out.astype(jnp.float32), axis=1)
    ).astype(jnp.bfloat16)
    pair_grad = join_back(back_grad)[place_bwd].reshape(tokens_here, TOP, feature_count)
    feature_grad = jnp.sum(pair_grad.astype(jnp.float32), axis=1)
    scaled = gain_row * feature_grad
    mean_term = jnp.mean(saved_values * scaled, axis=-1, keepdims=True)
    bwd_out = (grad_values + saved_inv * scaled - saved_values * saved_inv**3 * mean_term).astype(
        jnp.bfloat16
    )
    local_gain = jnp.sum(feature_grad * saved_values * saved_inv, axis=0)
    section_gain = lax.psum(local_gain, "ep")
    mirrored = section_gain
    for bit_index in range(lax.axis_size("pp").bit_length() - 1):
        mirrored = partner_2(mirrored, "pp", bit_index)
    gain_grad = (section_gain + mirrored)[None]
    return (fwd_out[None], bwd_out[None], gain_grad)


def solution(mesh):
    placed = (
        P("pp", "ep", None),
        P("pp", "ep", None),
        P("pp", "ep", None),
        P("pp", "ep", None, None),
        P("pp", "ep", None),
        P("pp", "ep", None),
        P("pp", "ep", None),
        P("pp", "ep", None),
        P("pp", None),
        P("pp", "ep", None),
        P("pp", None, "ep"),
    )
    return jax.shard_map(
        on_device,
        mesh=mesh,
        in_specs=placed,
        out_specs=(P("pp", "ep", None), P("pp", "ep", None), P("pp", None)),
        check_vma=False,
    )
```

profile of v0, /device:TPU:16, one launch (start us, length us, event | category | flops | bytes accessed | tf_op | source)
XLA Modules:
  0.0 894.3 jit_solution(3430475854433938393)
XLA Ops:
  0.6 1.4 collective-permute-start.3
  6.7 1.4 scatter_custom_fusion.1
  8.1 34.6 %collective-permute-done.3 = bf16[1,128,7168]{2,1,0:T(8,128)(2,1)S(1)} collective-permute-done((bf16[1,128,7168]{2,1,0:T(8,128)(2,1)}, bf16[1,128,7168]{2,1,0:T(8,128)(2,1)S(1)}, u32[]{:S(2)}, u32[]{:S(2)}) %collective-permute-start.3) | collective-permute-done | bytes 1835040 | tf_op jit(solution)/shard_map/ppermute | solution.py:18
  43.0 4.2 mul.194
  47.2 9.5 %mul.195 = f32[256,7168]{1,0:T(8,128)} reshape(f32[128,2,7168]{2,1,0:T(2,128)} %mul.194) | data formatting | bytes 14680064 | tf_op jit(solution)/shard_map/mul | solution.py:94
  56.8 3.9 multiply_convert_fusion
  60.6 2.3 concatenate.10
  62.9 15.3 %gather_fusion.2 = bf16[288,7168]{1,0:T(8,128)(2,1)} fusion(bf16[257,7168]{1,0:T(8,128)(2,1)} %concatenate.10, s32[1024]{0:T(1024)S(1)} %pad_clamp_fusion.1), kind=kCustom, calls=%fused_computation.2 | custom fusion | bytes 8258688 | tf_op jit(solution)/shard_map/gather | solution.py:69
  78.2 8.4 reshape.283
  86.7 4.6 copy.37
  91.3 8.3 all-to-all-start.2
  100.1 2.4 gather_fusion.3
  102.6 51.6 %all-to-all-done.2 = bf16[16,72,1792]{2,1,0:T(8,128)(2,1)} async-done(((bf16[16,72,1792]{2,1,0:T(8,128)(2,1)}), bf16[16,72,1792]{2,1,0:T(8,128)(2,1)}, u32[]{:S(2)}, u32[]{:S(2)}) %all-to-all-start.2) | async-done | bytes 4128800 | tf_op jit(solution)/shard_map/all_to_all | solution.py:127
  154.1 2.7 broadcast_in_dim.16
  156.9 12.6 %all-to-all-start.3 = ((bf16[16,72,2048]{2,1,0:T(8,128)(2,1)}), bf16[16,72,2048]{2,1,0:T(8,128)(2,1)}, u32[]{:S(2)}, u32[]{:S(2)}) async-start(bf16[16,72,2048]{2,1,0:T(8,128)(2,1)} %bitcast.148), calls=%async_computation.3 | async-start | bytes 9437184 | tf_op jit(solution)/shard_map/all_to_all | solution.py:128
  169.5 7.8 convolution_convert_fusion.3
  177.7 4.2 collective-permute-done.4
  183.0 2.4 collective-permute-start.5
  185.4 46.9 %all-to-all-done.3 = bf16[16,72,2048]{2,1,0:T(8,128)(2,1)} async-done(((bf16[16,72,2048]{2,1,0:T(8,128)(2,1)}), bf16[16,72,2048]{2,1,0:T(8,128)(2,1)}, u32[]{:S(2)}, u32[]{:S(2)}) %all-to-all-start.3) | async-done | bytes 4718624 | tf_op jit(solution)/shard_map/all_to_all | solution.py:128
  232.3 12.9 %reshape.294 = f32[1152,2,1024]{2,1,0:T(2,128)} reshape(bf16[16,72,2048]{2,1,0:T(8,128)(2,1)} %all-to-all-done.3) | data formatting | bytes 14155776 | tf_op jit(solution)/shard_map/convert_element_type | solution.py:144
  245.2 10.7 %fusion.40 = (f32[1152,1,1024]{2,1,0:T(1,128)S(1)}, f32[1152,1,1024]{2,1,0:T(1,128)S(1)}) fusion(f32[1152,2,1024]{2,1,0:T(2,128)} %reshape.294), kind=kLoop, calls=%fused_computation.91 | loop fusion | bytes 18874368 | tf_op jit(solution)/shard_map/slice | solution.py:146
  255.9 23.9 %collective-permute-done.5 = bf16[1152,1024]{1,0:T(8,128)(2,1)} collective-permute-done((bf16[1152,1024]{1,0:T(8,128)(2,1)S(1)}, bf16[1152,1024]{1,0:T(8,128)(2,1)}, u32[]{:S(2)}, u32[]{:S(2)}) %collective-permute-start.5) | collective-permute-done | bytes 2359328 | tf_op jit(solution)/shard_map/ppermute | solution.py:24
  279.8 4.7 fusion.28
  284.5 2.6 pad_maximum_fusion
  287.1 6.8 copy.40
  293.8 15.1 %convolution_convert_fusion.1 = bf16[1152,1792]{1,0:T(8,128)(2,1)} fusion(bf16[1152,2048]{0,1:T(8,128)(2,1)} %bitcast.153, bf16[1,1792,2048]{2,1,0:T(8,128)(2,1)} %param.20), kind=kOutput, calls=%fused_computation.10 | convolution fusion | flops 8457781248 | bytes 16187392 | tf_op jit(solution)/shard_map/dot_general | solution.py:149
  309.0 4.7 all-to-all-start.4
  316.4 1.6 scatter_custom_fusion
  318.0 1.9 fusion.17
  320.0 87.6 %collective-permute-done = bf16[1,128,7168]{2,1,0:T(8,128)(2,1)S(1)} collective-permute-done((bf16[1,128,7168]{2,1,0:T(8,128)(2,1)}, bf16[1,128,7168]{2,1,0:T(8,128)(2,1)S(1)}, u32[]{:S(2)}, u32[]{:S(2)}) %collective-permute-start) | collective-permute-done | bytes 1835040 | tf_op jit(solution)/shard_map/ppermute | solution.py:18
  408.1 3.8 copy.41
  411.8 2.6 copy.49
  414.4 10.8 %gather_fusion.4 = bf16[256,7168]{1,0:T(8,128)(2,1)} fusion(bf16[288,7168]{1,0:T(8,128)(2,1)} %bitcast.146, s32[1024]{0:T(1024)S(1)} %pad_clamp_fusion), kind=kCustom, calls=%fused_computation.4 | custom fusion | bytes 7341056 | tf_op jit(solution)/shard_map/gather | solution.py:163
  425.2 8.8 reshape.295
  434.1 12.3 %reduce_sum.88 = f32[128,7168]{1,0:T(8,128)} reduce(f32[128,2,7168]{2,1,0:T(2,128)} %reshape.295, f32[]{:T(128)} %constant.10.clone.1), dimensions={1}, to_apply=%region_11.12 | reduce | flops 917504 | bytes 11010052 | tf_op jit(solution)/shard_map/reduce_sum | solution.py:164
  446.4 4.4 fusion.20
  450.8 3.3 broadcast_in_dim.12
  454.2 8.4 reshape.273
  462.6 4.4 concatenate.9
  466.9 15.7 %gather_fusion = bf16[288,7168]{1,0:T(8,128)(2,1)} fusion(bf16[257,7168]{1,0:T(8,128)(2,1)} %concatenate.9, s32[1024]{0:T(1024)S(1)} %pad_clamp_fusion.3), kind=kCustom, calls=%fused_computation | custom fusion | bytes 8258688 | tf_op jit(solution)/shard_map/gather | solution.py:69
  482.6 8.4 reshape.275
  491.1 2.8 copy.27
  493.9 60.8 %all_to_all.25 = bf16[16,72,1792]{2,1,0:T(8,128)(2,1)S(1)} all-to-all(bf16[16,72,1792]{2,1,0:T(8,128)(2,1)S(1)} %bitcast.151), channel_id=1, replica_groups=mesh['pp'=8,'ep'=16] {'ep'}, dimensions={0} | all-to-all | bytes 8257536 | tf_op jit(solution)/shard_map/all_to_all | solution.py:106
  554.8 9.1 %convolution_convert_fusion.2 = bf16[1152,2048]{1,0:T(8,128)(2,1)S(1)} fusion(bf16[1152,1792]{1,0:T(8,128)(2,1)S(1)} %bitcast.157, bf16[1,1792,2048]{2,1,0:T(8,128)(2,1)S(1)} %bitcast.171), kind=kOutput, calls=%fused_computation.11 | convolution fusion | flops 8458076160 | bytes 16187392 | tf_op jit(solution)/shard_map/dot_general | solution.py:108
  564.1 7.9 collective-permute-done.1
  572.0 2.6 add_convert_fusion
  574.7 103.8 %collective-permute-done.2 = bf16[1152,2048]{1,0:T(8,128)(2,1)S(1)} collective-permute-done((bf16[1152,2048]{1,0:T(8,128)(2,1)S(1)}, bf16[1152,2048]{1,0:T(8,128)(2,1)S(1)}, u32[]{:S(2)}, u32[]{:S(2)}) %collective-permute-start.2) | collective-permute-done | bytes 4718624 | tf_op jit(solution)/shard_map/ppermute | solution.py:24
  678.6 5.8 convert_add_fusion
  684.4 13.2 %reshape.278 = f32[1152,2,1024]{2,1,0:T(2,128)} reshape(f32[1152,2048]{1,0:T(8,128)} %convert_add_fusion) | data formatting | bytes 18874368 | tf_op jit(solution)/shard_map/reshape | solution.py:118
  697.6 11.2 %fusion.41 = (f32[1152,1,1024]{2,1,0:T(1,128)S(1)}, f32[1152,1,1024]{2,1,0:T(1,128)S(1)}) fusion(f32[1152,2,1024]{2,1,0:T(2,128)} %reshape.278), kind=kLoop, calls=%fused_computation.92 | loop fusion | bytes 18874368 | tf_op jit(solution)/shard_map/slice | solution.py:120
  708.8 6.9 convolution_convert_fusion
  715.7 4.7 all-to-all-start.1
  720.4 116.5 %psum.7 = f32[7168]{0:T(1024)S(1)} all-reduce(f32[7168]{0:T(1024)S(1)} %get-tuple-element.3), channel_id=1, replica_groups=mesh['pp'=8,'ep'=16] {'ep'}, use_global_device_ids=true, to_apply=%region_14.15 | all-reduce | flops 7168 | bytes 57344 | tf_op jit(solution)/shard_map/psum | solution.py:171
  837.1 3.7 collective-permute-done.6
  840.8 1.6 collective-permute-start.7
  842.4 2.3 collective-permute-done.7
  844.7 4.3 collective-permute-start.8
  849.0 5.9 fusion.16
  855.5 3.8 copy.30
  859.3 2.6 copy.47
  861.9 10.8 %gather_fusion.1 = bf16[256,7168]{1,0:T(8,128)(2,1)} fusion(bf16[288,7168]{1,0:T(8,128)(2,1)} %bitcast.147, s32[1024]{0:T(1024)S(1)} %pad_clamp_fusion.2), kind=kCustom, calls=%fused_computation.1 | custom fusion | bytes 7341056 | tf_op jit(solution)/shard_map/gather | solution.py:159
  872.7 8.8 reshape.291
  881.5 10.8 %multiply_reduce_fusion = f32[128,7168]{1,0:T(8,128)S(1)} fusion(f32[128,2,7168]{2,1,0:T(2,128)} %reshape.291, f32[128,2]{1,0:T(8,128)S(1)} %copy.21), kind=kLoop, calls=%fused_computation.15 | loop fusion | flops 2752512 | bytes 11011072 | tf_op jit(solution)/shard_map/reduce_sum | solution.py:161
  892.3 1.6 fusion.14
  (77 shorter events, 11.3 us)
Async XLA Ops:
  0.6 42.0 %collective-permute-start.3 = (bf16[1,128,7168]{2,1,0:T(8,128)(2,1)}, bf16[1,128,7168]{2,1,0:T(8,128)(2,1)S(1)}, u32[]{:S(2)}, u32[]{:S(2)}) collective-permute-start(bf16[1,128,7168]{2,1,0:T(8,128)(2,1)} %param.12), channel_id=1, source_target_pairs={{16,0},{32,16},{48,32},{64,48},{80,64},{96,80},{112,96},{0,112},{1... | collective-permute-start | bytes 5505032 | tf_op jit(solution)/shard_map/ppermute | solution.py:18
  42.7 4.6 copy-start
  91.3 8.3 copy-start.1
  91.3 62.9 %all-to-all-start.2 = ((bf16[16,72,1792]{2,1,0:T(8,128)(2,1)}), bf16[16,72,1792]{2,1,0:T(8,128)(2,1)}, u32[]{:S(2)}, u32[]{:S(2)}) async-start(bf16[16,72,1792]{2,1,0:T(8,128)(2,1)} %bitcast.149), calls=%async_computation.2 | async-start | bytes 8257536 | tf_op jit(solution)/shard_map/all_to_all | solution.py:127
  156.9 75.4 %all-to-all-start.3 = ((bf16[16,72,2048]{2,1,0:T(8,128)(2,1)}), bf16[16,72,2048]{2,1,0:T(8,128)(2,1)}, u32[]{:S(2)}, u32[]{:S(2)}) async-start(bf16[16,72,2048]{2,1,0:T(8,128)(2,1)} %bitcast.148), calls=%async_computation.3 | async-start | bytes 9437184 | tf_op jit(solution)/shard_map/all_to_all | solution.py:128
  177.3 4.6 collective-permute-start.4
  183.0 96.8 %collective-permute-start.5 = (bf16[1152,1024]{1,0:T(8,128)(2,1)S(1)}, bf16[1152,1024]{1,0:T(8,128)(2,1)}, u32[]{:S(2)}, u32[]{:S(2)}) collective-permute-start(bf16[1152,1024]{1,0:T(8,128)(2,1)S(1)} %add_convert_fusion.1), channel_id=1, source_target_pairs={{0,2},{1,3},{2,0},{3,1},{4,6},{5,7},{6,4},{7,5},{8,10},{9,11},{10,... | collective-permute-start | bytes 7077896 | tf_op jit(solution)/shard_map/ppermute | solution.py:24
  309.0 5.1 copy-start.3
  309.0 99.1 %all-to-all-start.4 = ((bf16[16,72,1792]{2,1,0:T(8,128)(2,1)}), bf16[16,72,1792]{2,1,0:T(8,128)(2,1)}, u32[]{:S(2)}, u32[]{:S(2)}) async-start(bf16[16,72,1792]{2,1,0:T(8,128)(2,1)} %bitcast.155), calls=%async_computation.4 | async-start | bytes 8257536 | tf_op jit(solution)/shard_map/all_to_all | solution.py:158
  313.7 93.9 %collective-permute-start = (bf16[1,128,7168]{2,1,0:T(8,128)(2,1)}, bf16[1,128,7168]{2,1,0:T(8,128)(2,1)S(1)}, u32[]{:S(2)}, u32[]{:S(2)}) collective-permute-start(bf16[1,128,7168]{2,1,0:T(8,128)(2,1)} %param.11), channel_id=1, source_target_pairs={{112,0},{0,16},{16,32},{32,48},{48,64},{64,80},{80,96},{96,112},{1... | collective-permute-start | bytes 5505032 | tf_op jit(solution)/shard_map/ppermute | solution.py:18
  434.1 12.3 %copy-start.2 = (f32[1,7168]{1,0:T(1,128)S(1)}, f32[1,7168]{1,0:T(1,128)}, u32[]{:S(2)}) copy-start(f32[1,7168]{1,0:T(1,128)} %param.19) | copy-start | bytes 86020
  491.1 63.7 %slice-start = ((s8[7340032]{0:T(1024)(128)(4,1)}), s8[4194304]{0:T(1024)(128)(4,1)S(1)}, s32[]{:S(2)}) async-start(s8[7340032]{0:T(1024)(128)(4,1)} %bitcast.170), calls=%async_computation.5 | async-start | bytes 8388608
  493.9 60.9 %slice-start.1 = ((s8[7340032]{0:T(1024)(128)(4,1)}), s8[3145728]{0:T(1024)(128)(4,1)S(1)}, s32[]{:S(2)}) async-start(s8[7340032]{0:T(1024)(128)(4,1)} %bitcast.170), calls=%async_computation.6 | async-start | bytes 6291456
  563.8 8.2 collective-permute-start.1
  574.6 103.9 %collective-permute-start.2 = (bf16[1152,2048]{1,0:T(8,128)(2,1)S(1)}, bf16[1152,2048]{1,0:T(8,128)(2,1)S(1)}, u32[]{:S(2)}, u32[]{:S(2)}) collective-permute-start(bf16[1152,2048]{1,0:T(8,128)(2,1)S(1)} %add_convert_fusion), channel_id=1, source_target_pairs={{0,2},{1,3},{2,0},{3,1},{4,6},{5,7},{6,4},{7,5},{8,10},{9,11},{10,... | collective-permute-start | bytes 14155784 | tf_op jit(solution)/shard_map/ppermute | solution.py:24
  697.6 11.2 %copy-start.5 = (bf16[1,1024,1792]{2,1,0:T(8,128)(2,1)S(1)}, bf16[1,1024,1792]{2,1,0:T(8,128)(2,1)}, u32[]{:S(2)}) copy-start(bf16[1,1024,1792]{2,1,0:T(8,128)(2,1)} %param.21) | copy-start | bytes 11010052
  715.7 121.2 %copy-start.4 = (f32[1,128,2]{1,2,0:T(2,128)S(1)}, f32[1,128,2]{1,2,0:T(2,128)}, u32[]{:S(2)}) copy-start(f32[1,128,2]{1,2,0:T(2,128)} %param.17) | copy-start | bytes 3076
  715.7 139.8 %all-to-all-start.1 = ((bf16[16,72,1792]{2,1,0:T(8,128)(2,1)}), bf16[16,72,1792]{2,1,0:T(8,128)(2,1)}, u32[]{:S(2)}, u32[]{:S(2)}) async-start(bf16[16,72,1792]{2,1,0:T(8,128)(2,1)} %bitcast.156), calls=%async_computation.1 | async-start | bytes 8257536 | tf_op jit(solution)/shard_map/all_to_all | solution.py:125
  836.9 3.9 collective-permute-start.6
  840.8 3.9 collective-permute-start.7
  844.7 10.2 %collective-permute-start.8 = (f32[7168]{0:T(1024)S(1)}, f32[7168]{0:T(1024)S(1)}, u32[]{:S(2)}, u32[]{:S(2)}) collective-permute-start(f32[7168]{0:T(1024)S(1)} %collective-permute-done.7), channel_id=1, source_target_pairs={{0,64},{16,80},{32,96},{48,112},{64,0},{80,16},{96,32},{112,48},{1... | collective-permute-start | bytes 86024 | tf_op jit(solution)/shard_map/ppermute | solution.py:24
where the time goes:
time: 906 us; the launch traced here: 894 us
  waiting for transfers between devices  367 us (41%)
  local copies, waits for them, and re-layouts  206 us (23%)
  blocking collectives  177 us (20%)
  other arithmetic  62.5 us (7%)
  starting transfers between devices  41.2 us (5%)
  matrix products  38.8 us (4%)
    ppermute x7, waiting for transfers between devices, partner_2(): return lax.ppermute(value, axis, pairs)  146 us
    ppermute x2, waiting for transfers between devices, shifted(): return lax.ppermute(block, axis, route)  122 us
    psum x1, blocking collectives, on_device(): section_gain = lax.psum(local_gain, 'ep')  117 us
    all_to_all x1, blocking collectives, on_device(): lax.all_to_all(send_rows, 'ep', split_axis=0, concat_axis=0, tiled=True)  60.8 us
    all_to_all x1, waiting for transfers between devices, on_device(): lax.all_to_all(send_grad, 'ep', split_axis=0, concat_axis=0, tiled=True)  51.6 us
    all_to_all x1, waiting for transfers between devices, on_device(): lax.all_to_all(send_pre, 'ep', split_axis=0, concat_axis=0, tiled=True)  46.9 us
    gather x3, local copies, waits for them, and re-layouts, outbound(): return padded[inverse]  33.4 us
    reshape x4, local copies, waits for them, and re-layouts, split_send(): rows.reshape(EXPERTS, CAP, slices, piece_width).transpose(0, 2, 1, 3)  24.3 us
  transfers between devices with their start and end apart: 13, of which 10 were waited for; matrix products, arithmetic and copies ran while one was open for 6% of the time, Pallas kernels for 0%

commit v1 on v0

v1 whole, which is shorter than its diff:
```python
import jax
import jax.numpy as jnp
from jax import lax
from jax.experimental import pallas as pl
from jax.experimental.pallas import tpu as pltpu
from jax.sharding import PartitionSpec as P

D = 7168
FF = 1024
CAP = 72
TOK = 128
SLICE = 1792
ROWS = 2 * CAP
TILE = 256
EPS = 1e-06
F32 = jnp.float32
BF16 = jnp.bfloat16
MESH = pl.DeviceIdType.MESH


def kernel(
    meta,
    gain,
    fwd_sent,
    bwd_sent,
    saved,
    pre,
    w_in,
    w_out,
    fwd_out,
    bwd_out,
    local_gain,
    ret_f,
    ret_b,
    w1,
    w2,
    v_f,
    v_b,
    x_f,
    x_b,
    s_f,
    s_b,
    part,
    r1_f,
    r1_b,
    r2_f,
    r2_b,
    h_f,
    h_b,
    xr_f,
    xr_b,
    pre_in,
    pre_out,
    pre_got,
    stage,
    meta_got,
    inv_out,
    inv_got,
    pick_f,
    pick_b,
    pick_pre,
    comb_f,
    comb_b,
    load_sem,
    stage_sem,
    out_sem,
    misc_send,
    misc_recv,
    pre_send,
    pre_recv,
    s1_send,
    s1_recv,
    d_send,
    d_recv,
    r1_send,
    r1_recv,
    r2_send,
    r2_recv,
    ag_send,
    ag_recv,
    ac_send,
    ac_recv,
    ret_send,
    ret_recv,
    x_send,
    x_recv,
):
    p = lax.axis_index("pp")
    ep = lax.axis_index("ep")
    xh = ep // 8
    z = (ep // 2) % 4
    c = ep % 2
    zp = z % 2
    own_row = pl.multiple_of(xh * TOK, TOK)
    other_row = pl.multiple_of((1 - xh) * TOK, TOK)

    def place(dp, dx, dz, dc):
        x2 = (xh + dx) % 2
        z2 = (z + dz) % 4
        c2 = (c + dc) % 2
        return {"pp": (p + dp) % 8, "ep": x2 * 8 + z2 * 2 + c2}

    def remote(src, dst, send, recv, target):
        return pltpu.make_async_remote_copy(
            src_ref=src,
            dst_ref=dst,
            send_sem=send,
            recv_sem=recv,
            device_id=target,
            device_id_type=MESH,
        )

    def columns(dz, dc):
        j = 2 * ((z + dz) % 2) + (c + dc) % 2
        return pl.multiple_of(j * SLICE, TILE)

    pairs = [(0, 1), (1, 0), (1, 1), (0, 0)]

    loads = []
    for q in range(4):
        loads.append(
            pltpu.make_async_copy(
                fwd_sent.at[:, pl.ds(q * SLICE, SLICE)], s_f.at[q, pl.ds(0, TOK)], load_sem.at[q]
            )
        )
    loads.append(pltpu.make_async_copy(pre, pre_in, load_sem.at[4]))
    loads.append(pltpu.make_async_copy(w_in, w1, load_sem.at[5]))
    loads.append(pltpu.make_async_copy(w_out, w2, load_sem.at[6]))
    for load in loads:
        load.start()

    peers = [(1, 0, 0, 0), (1, 1, 0, 0), (7, 0, 0, 0), (7, 1, 0, 0), (0, 1, 0, 0), (0, 1, 2, 0)]
    peers += [(0, 0, dz, dc) for dz in range(4) for dc in range(2) if (dz, dc) != (0, 0)]
    barrier = pltpu.get_barrier_semaphore()
    for peer in peers:
        pl.semaphore_signal(barrier, inc=1, device_id=place(*peer), device_id_type=MESH)
    pl.semaphore_wait(barrier, len(peers))

    meta_copy = remote(meta, meta_got, misc_send.at[0], misc_recv.at[0], place(0, 1, 0, 0))
    meta_copy.start()

    def sent_copies(stream, src, dst, dp):
        made = {}
        for dz, dc in pairs:
            cols = pl.ds(columns(dz, dc), SLICE)
            for dx in range(2):
                made[dz, dc, dx] = remote(
                    src.at[:, cols],
                    dst.at[pl.ds(own_row, TOK), cols],
                    s1_send.at[stream, 2 * dz + dc, dx],
                    s1_recv.at[stream, 2 * dz + dc, dx],
                    place(dp, dx, 0, 0),
                )
        return made

    first_f = sent_copies(0, fwd_sent, v_f, 1)
    first_b = sent_copies(1, bwd_sent, v_b, 7)
    for copy in first_f.values():
        copy.start()

    total = jnp.zeros((TOK, 1), F32)
    for q in range(4):
        loads[q].wait()
        block = s_f[q, pl.ds(0, TOK), :].astype(F32)
        total = total + jnp.sum(block * block, axis=1, keepdims=True)
    inv_out[...] = jnp.broadcast_to(lax.rsqrt(total / D + EPS), (TOK, 128))
    inv_copies = [
        remote(
            inv_out,
            inv_got.at[pl.ds(own_row, TOK)],
            misc_send.at[1 + dx],
            misc_recv.at[1 + dx],
            place(1, dx, 0, 0),
        )
        for dx in range(2)
    ]
    for copy in inv_copies:
        copy.start()
    for copy in first_b.values():
        copy.start()

    meta_copy.wait_recv()
    own_meta = meta[...]
    got_meta = meta_got[...]
    row_id = lax.broadcasted_iota(jnp.int32, (TOK, TOK), 0)
    col_id = lax.broadcasted_iota(jnp.int32, (TOK, TOK), 1)
    before = jnp.where(row_id < col_id, 1.0, 0.0).astype(BF16)

    def slots(block, stream, expert):
        expert = expert.astype(F32)
        hit0 = jnp.where(block[2 * stream : 2 * stream + 1] == expert, 1.0, 0.0)
        hit1 = jnp.where(block[2 * stream + 1 : 2 * stream + 2] == expert, 1.0, 0.0)
        hit = hit0 + hit1
        wide = jnp.broadcast_to(hit, (16, TOK)).astype(BF16)
        slot = jnp.dot(wide, before, preferred_element_type=F32)[0:1]
        gate = (
            block[4 + 2 * stream : 5 + 2 * stream] * hit0
            + block[5 + 2 * stream : 6 + 2 * stream] * hit1
        )
        return hit0, hit1, hit, slot, gate

    for stream, pick, comb in ((0, pick_f, comb_f), (1, pick_b, comb_b)):
        rows_needed = []
        for local in range(2):
            expert = 2 * xh + local
            own = slots(own_meta, stream, expert)
            got = slots(got_meta, stream, expert)
            low = xh == 0
            hit_row = jnp.concatenate(
                [jnp.where(low, own[2], got[2]), jnp.where(low, got[2], own[2])], axis=1
            )
            slot_row = jnp.concatenate(
                [jnp.where(low, own[3], got[3]), jnp.where(low, got[3], own[3]) + CAP], axis=1
            )
            line = lax.broadcasted_iota(jnp.int32, (ROWS, 2 * TOK), 0).astype(F32)
            pick[local] = jnp.where((line == slot_row) & (hit_row > 0.5), 1.0, 0.0).astype(BF16)
            for side in (own, got):
                rows_needed += [side[3], side[4]]
        padding = jnp.zeros((TOK - len(rows_needed), TOK), F32)
        turned = jnp.concatenate(rows_needed + [padding], axis=0).T
        lane = lax.broadcasted_iota(jnp.int32, (TOK, 2 * ROWS), 1).astype(F32)
        for side in range(2):
            home = jnp.where(xh == 0, side, 1 - side).astype(F32)
            mix = jnp.zeros((TOK, 2 * ROWS), F32)
            for local in range(2):
                k = 2 * (2 * local + side)
                slot_col = turned[:, k : k + 1] + (home * CAP + local * ROWS)
                gate_col = turned[:, k + 1 : k + 2]
                mix = mix + jnp.where(lane == slot_col, gate_col, 0.0)
            high = mix.astype(BF16)
            comb[pl.ds(2 * side * TOK, TOK), :] = high
            comb[pl.ds((2 * side + 1) * TOK, TOK), :] = (mix - high.astype(F32)).astype(BF16)

    loads[4].wait()
    pre_copies = {}
    for dx in range(2):
        for i in range(2):
            expert = 2 * ((xh + dx) % 2) + ((z + 2 * i) % 4) // 2
            hit0, hit1, _, slot, _ = slots(own_meta, 1, expert)
            hit_row = jnp.concatenate([hit0, hit1], axis=1)
            slot_row = jnp.concatenate([slot, slot], axis=1)
            line = lax.broadcasted_iota(jnp.int32, (80, 2 * TOK), 0).astype(F32)
            pick_pre[...] = jnp.where((line == slot_row) & (hit_row > 0.5), 1.0, 0.0).astype(BF16)
            target = pre_got.at[i, xh] if (dx, i) == (0, 0) else pre_out.at[2 * dx + i]

            def gather_pre(t, carry, target=target):
                cols = pl.ds(pl.multiple_of(t * 512, 512), 512)
                target[:, cols] = jnp.dot(
                    pick_pre[...], pre_in[:, cols], preferred_element_type=F32
                ).astype(BF16)
                return carry

            lax.fori_loop(0, 4, gather_pre, 0)
            if (dx, i) != (0, 0):
                copy = remote(
                    pre_out.at[2 * dx + i],
                    pre_got.at[i, xh],
                    pre_send.at[i, dx],
                    pre_recv.at[i, dx],
                    place(0, dx, 2 * i, 0),
                )
                copy.start()
                pre_copies[dx, i] = copy

    def dispatch(stream, first, v, pick, s, x):
        made = {}
        for dzp, dc in pairs:
            for dx in range(2):
                first[dzp, dc, dx].wait_recv()
            base = columns(dzp, dc)
            outs = []
            for dz in (dzp, dzp + 2):
                here = x if (dz, dc) == (0, 0) else s
                outs.append((here, dz, ((z + dz) % 4) // 2))

            def gather(t, carry, base=base, outs=outs, dc=dc):
                cols = pl.ds(pl.multiple_of(base + t * TILE, TILE), TILE)
                block = v[:, cols]
                if stream == 0:
                    block = (block.astype(F32) * inv_got[:, 0:1] * gain[:, cols]).astype(BF16)
                where = pl.ds(pl.multiple_of(t * TILE, TILE), TILE)
                for ref, dz, local in outs:
                    ref[dz, pl.ds(dc * ROWS, ROWS), where] = jnp.dot(
                        pick[local], block, preferred_element_type=F32
                    ).astype(BF16)
                return carry

            lax.fori_loop(0, SLICE // TILE, gather, 0)
            for dz in (dzp, dzp + 2):
                if (dz, dc) == (0, 0):
                    continue
                rows = pl.ds(dc * ROWS, ROWS)
                copy = remote(
                    s.at[dz, rows],
                    x.at[dz, rows],
                    d_send.at[stream, dz, dc],
                    d_recv.at[stream, dz, dc],
                    place(0, 0, dz, dc),
                )
                copy.start()
                made[dz, dc] = copy
        return made

    def multiply(lhs, w, out, count, tile, turned):
        def step(t, carry):
            cols = pl.ds(pl.multiple_of(t * tile, tile), tile)
            if turned:
                got = lax.dot_general(
                    lhs[...], w[cols, :], (((1,), (1,)), ((), ())), preferred_element_type=F32
                )
            else:
                got = jnp.dot(lhs[...], w[:, cols], preferred_element_type=F32)
            out[:, cols] = got.astype(BF16)
            return carry

        lax.fori_loop(0, count // tile, step, 0)

    def first_products(stream, sent, x, r1, width):
        made = []
        for dz in range(4):
            for dc in range(2):
                if (dz, dc) != (0, 0):
                    sent[dz, dc].wait_recv()
            out = part.at[dz, :, pl.ds(0, width)]
            if stream == 0:
                multiply(x.at[dz], w1, out, width, 512, False)
            else:
                multiply(x.at[dz], w2, out, width, 512, True)
            copy = remote(
                part.at[dz, pl.ds(ROWS, ROWS), pl.ds(0, width)],
                r1.at[dz],
                r1_send.at[stream, dz],
                r1_recv.at[stream, dz],
                place(0, 0, 0, 1),
            )
            copy.start()
            made.append(copy)
        return made

    partner = {"pp": p, "ep": xh * 8 + (z + 1 - 2 * zp) * 2 + c}

    def chip_sums(stream, crossed, r1, r2, width):
        made = []
        for dz in (1, 3, 0, 2):
            crossed[dz].wait_recv()

            def add(t, carry, dz=dz):
                cols = pl.ds(pl.multiple_of(t * 512, 512), 512)
                rows = pl.ds(0, ROWS)
                part[dz, rows, cols] = (
                    part[dz, rows, cols].astype(F32) + r1[dz, :, cols].astype(F32)
                ).astype(BF16)
                return carry

            lax.fori_loop(0, width // 512, add, 0)
            if dz % 2 == 1:
                index = ((dz + 5 - 2 * zp) % 4) // 2
                copy = remote(
                    part.at[dz, pl.ds(0, ROWS), pl.ds(0, width)],
                    r2.at[index],
                    r2_send.at[stream, dz // 2],
                    r2_recv.at[stream, index],
                    partner,
                )
                copy.start()
                made.append(copy)
        return made

    def landed(stream, r2, width, index):
        return remote(
            part.at[0, pl.ds(0, ROWS), pl.ds(0, width)],
            r2.at[index],
            r2_send.at[stream, 0],
            r2_recv.at[stream, index],
            partner,
        )

    def activate(stream, r2, h, width):
        partner_copies, core_copies = [], {}
        rows = pl.ds(0, ROWS)
        for i in range(2):
            dz = 2 * i
            landed(stream, r2, width, i).wait_recv()
            if stream == 1:
                for dx in range(2):
                    if (dx, i) != (0, 0):
                        pre_copies[dx, i].wait_recv()

            def step(t, carry, i=i, dz=dz):
                lo = pl.ds(pl.multiple_of(t * TILE, TILE), TILE)
                hi = pl.ds(pl.multiple_of(t * TILE + FF, TILE), TILE)
                if stream == 0:
                    g = part[dz, rows, lo].astype(F32) + r2[i, :, lo].astype(F32)
                    u = part[dz, rows, hi].astype(F32) + r2[i, :, hi].astype(F32)
                    h[dz, rows, lo] = (g / (1.0 + jnp.exp(-g)) * u).astype(BF16)
                else:
                    hg = part[dz, rows, lo].astype(F32) + r2[i, :, lo].astype(F32)
                    g = jnp.concatenate(
                        [pre_got[i, k, :, lo].astype(F32)[0:CAP] for k in range(2)], axis=0
                    )
                    u = jnp.concatenate(
                        [pre_got[i, k, :, hi].astype(F32)[0:CAP] for k in range(2)], axis=0
                    )
                    sig = 1.0 / (1.0 + jnp.exp(-g))
                    h[dz, rows, lo] = (hg * u * sig * (1.0 + g * (1.0 - sig))).astype(BF16)
                    h[dz, rows, hi] = (hg * g * sig).astype(BF16)
                return carry

            lax.fori_loop(0, FF // TILE, step, 0)
            there = (dz + 5 - 2 * zp) % 4
            copy = remote(
                h.at[dz, rows],
                h.at[there, rows],
                ag_send.at[stream, i],
                ag_recv.at[stream, there // 2],
                partner,
            )
            copy.start()
            partner_copies.append(copy)
            core_copies[dz] = to_core(stream, h, dz)
            core_copies[dz].start()
        return partner_copies, core_copies

    def to_core(stream, h, dz):
        return remote(
            h.at[dz, pl.ds(0, ROWS)],
            h.at[dz, pl.ds(ROWS, ROWS)],
            ac_send.at[stream, dz],
            ac_recv.at[stream, dz],
            place(0, 0, 0, 1),
        )

    def forward_on(stream, h, core_copies):
        for i in range(2):
            dz = 2 * i + 1
            remote(
                h.at[2 * i, pl.ds(0, ROWS)],
                h.at[dz, pl.ds(0, ROWS)],
                ag_send.at[stream, i],
                ag_recv.at[stream, i],
                partner,
            ).wait_recv()
            core_copies[dz] = to_core(stream, h, dz)
            core_copies[dz].start()

    def second_products(stream, core_copies, h, s, ret):
        made = {}
        local = z // 2
        region = ret.at[
            pl.ds(pl.multiple_of(local * ROWS, ROWS), ROWS), pl.ds(columns(0, 0), SLICE)
        ]
        for dz in (0, 2, 1, 3):
            core_copies[dz].wait_recv()
            if stream == 0:
                multiply(h.at[dz], w2, s.at[dz], SLICE, TILE, False)
            else:
                multiply(h.at[dz], w1, s.at[dz], SLICE, TILE, True)
            for dc in range(2):
                rows = pl.ds(dc * ROWS, ROWS)
                if (dz, dc) == (0, 0):
                    copy = pltpu.make_async_copy(s.at[dz, rows], region, ret_recv.at[stream, 0, 0])
                else:
                    copy = remote(
                        s.at[dz, rows],
                        region,
                        ret_send.at[stream, dz, dc],
                        ret_recv.at[stream, dz, dc],
                        place(0, 0, 4 - dz, dc),
                    )
                copy.start()
                made[dz, dc] = copy
        return made

    def combine(stream, returned, ret, comb, v, x, xr):
        made = {}
        for n, (dzp, dc) in enumerate(pairs):
            for dz in (dzp, dzp + 2):
                if (dz, dc) == (0, 0):
                    returned[dz, dc].wait()
                else:
                    returned[dz, dc].wait_recv()
            base = columns(dzp, dc)
            fetch = pltpu.make_async_copy(
                ret.at[:, pl.ds(base, SLICE)], stage.at[n % 2], stage_sem.at[n % 2]
            )
            fetch.start()
            fetch.wait()
            jr = 2 * dzp + dc

            def step(t, carry, n=n, base=base, jr=jr):
                cols = pl.ds(pl.multiple_of(t * TILE, TILE), TILE)
                mixed = jnp.dot(comb[...], stage[n % 2, :, cols], preferred_element_type=F32)
                own = mixed[0:TOK] + mixed[TOK : 2 * TOK]
                other = mixed[2 * TOK : 3 * TOK] + mixed[3 * TOK :]
                high = own.astype(BF16)
                x[jr, pl.ds(0, TOK), cols] = high
                x[jr, pl.ds(TOK, TOK), cols] = (own - high.astype(F32)).astype(BF16)
                out_cols = pl.ds(pl.multiple_of(base + t * TILE, TILE), TILE)
                v[pl.ds(other_row, TOK), out_cols] = other.astype(BF16)
                return carry

            lax.fori_loop(0, SLICE // TILE, step, 0)
            copy = remote(
                v.at[pl.ds(other_row, TOK), pl.ds(base, SLICE)],
                xr.at[:, pl.ds(base, SLICE)],
                x_send.at[stream, jr],
                x_recv.at[stream, jr],
                place(0, 1, 0, 0),
            )
            copy.start()
            made[dzp, dc] = copy
        return made

    def finish_forward(crossed):
        for dzp, dc in pairs:
            crossed[dzp, dc].wait_recv()
            base = columns(dzp, dc)
            jr = 2 * dzp + dc

            def step(t, carry, base=base, jr=jr):
                cols = pl.ds(pl.multiple_of(t * TILE, TILE), TILE)
                wide = pl.ds(pl.multiple_of(base + t * TILE, TILE), TILE)
                here = pl.ds(own_row, TOK)
                mine = x_f[jr, pl.ds(0, TOK), cols].astype(F32)
                mine = mine + x_f[jr, pl.ds(TOK, TOK), cols].astype(F32)
                v_f[here, wide] = (
                    v_f[here, wide].astype(F32) + (mine + xr_f[:, wide].astype(F32))
                ).astype(BF16)
                return carry

            lax.fori_loop(0, SLICE // TILE, step, 0)
            copy = pltpu.make_async_copy(
                v_f.at[pl.ds(own_row, TOK), pl.ds(base, SLICE)],
                fwd_out.at[:, pl.ds(base, SLICE)],
                out_sem.at[0, jr],
            )
            copy.start()
            outs.append(copy)

    def finish_backward(crossed):
        total = jnp.zeros((TOK, 1), F32)
        for n, (dzp, dc) in enumerate(pairs):
            saved_loads[n].wait()
            block = s_f[2 * dzp + dc, pl.ds(0, TOK), :].astype(F32)
            total = total + jnp.sum(block * block, axis=1, keepdims=True)
        inv = lax.rsqrt(total / D + EPS)
        dots = jnp.zeros((TOK, TILE), F32)
        for dzp, dc in pairs:
            crossed[dzp, dc].wait_recv()
            base = columns(dzp, dc)
            jr = 2 * dzp + dc

            def step(t, carry, base=base, jr=jr):
                cols = pl.ds(pl.multiple_of(t * TILE, TILE), TILE)
                wide = pl.ds(pl.multiple_of(base + t * TILE, TILE), TILE)
                grad = x_b[jr, pl.ds(0, TOK), cols].astype(F32)
                grad = grad + x_b[jr, pl.ds(TOK, TOK), cols].astype(F32)
                grad = grad + xr_b[:, wide].astype(F32)
                high = grad.astype(BF16)
                x_b[jr, pl.ds(0, TOK), cols] = high
                x_b[jr, pl.ds(TOK, TOK), cols] = (grad - high.astype(F32)).astype(BF16)
                w = s_f[jr, pl.ds(0, TOK), cols].astype(F32)
                local_gain[:, wide] = jnp.sum(grad * w * inv, axis=0, keepdims=True)
                return carry + w * gain[:, wide] * grad

            dots = lax.fori_loop(0, SLICE // TILE, step, dots)
        scale = inv * inv * inv * (jnp.sum(dots, axis=1, keepdims=True) / D)
        for dzp, dc in pairs:
            base = columns(dzp, dc)
            jr = 2 * dzp + dc

            def last(t, carry, base=base, jr=jr):
                cols = pl.ds(pl.multiple_of(t * TILE, TILE), TILE)
                wide = pl.ds(pl.multiple_of(base + t * TILE, TILE), TILE)
                here = pl.ds(own_row, TOK)
                grad = x_b[jr, pl.ds(0, TOK), cols].astype(F32)
                grad = grad + x_b[jr, pl.ds(TOK, TOK), cols].astype(F32)
                w = s_f[jr, pl.ds(0, TOK), cols].astype(F32)
                v_b[here, wide] = (
                    v_b[here, wide].astype(F32) + inv * (gain[:, wide] * grad) - w * scale
                ).astype(BF16)
                return carry

            lax.fori_loop(0, SLICE // TILE, last, 0)
            copy = pltpu.make_async_copy(
                v_b.at[pl.ds(own_row, TOK), pl.ds(base, SLICE)],
                bwd_out.at[:, pl.ds(base, SLICE)],
                out_sem.at[1, jr],
            )
            copy.start()
            outs.append(copy)

    def sends_done(copies):
        for copy in copies:
            copy.wait_send()

    outs = []
    for copy in inv_copies:
        copy.wait_recv()
    sent_f = dispatch(0, first_f, v_f, pick_f, s_f, x_f)
    loads[5].wait()
    core_f = first_products(0, sent_f, x_f, r1_f, 2 * FF)
    chip_f = chip_sums(0, core_f, r1_f, r2_f, 2 * FF)
    sent_b = dispatch(1, first_b, v_b, pick_b, s_b, x_b)
    ag_f, ac_f = activate(0, r2_f, h_f, 2 * FF)
    loads[6].wait()
    forward_on(0, h_f, ac_f)
    sends_done(sent_f.values())
    back_f = second_products(0, ac_f, h_f, s_f, ret_f)
    sends_done(core_f + chip_f)
    core_b = first_products(1, sent_b, x_b, r1_b, FF)
    chip_b = chip_sums(1, core_b, r1_b, r2_b, FF)
    over_f = combine(0, back_f, ret_f, comb_f, v_f, x_f, xr_f)
    ag_b, ac_b = activate(1, r2_b, h_b, FF)
    forward_on(1, h_b, ac_b)
    sends_done(sent_b.values())
    back_b = second_products(1, ac_b, h_b, s_b, ret_b)
    sends_done([copy for key, copy in back_f.items() if key != (0, 0)])
    saved_loads = []
    for n, (dzp, dc) in enumerate(pairs):
        copy = pltpu.make_async_copy(
            saved.at[:, pl.ds(columns(dzp, dc), SLICE)],
            s_f.at[2 * dzp + dc, pl.ds(0, TOK)],
            load_sem.at[n],
        )
        copy.start()
        saved_loads.append(copy)
    finish_forward(over_f)
    over_b = combine(1, back_b, ret_b, comb_b, v_b, x_b, xr_b)
    finish_backward(over_b)

    sends_done([meta_copy] + inv_copies + list(pre_copies.values()))
    sends_done(list(first_f.values()) + list(first_b.values()))
    sends_done(core_b + chip_b + ag_f + ag_b)
    sends_done(list(ac_f.values()) + list(ac_b.values()))
    sends_done([copy for key, copy in back_b.items() if key != (0, 0)])
    sends_done(list(over_f.values()) + list(over_b.values()))
    for copy in outs:
        copy.wait()


def on_device(
    fwd_sent,
    bwd_sent,
    bwd_saved,
    bwd_pre,
    fwd_route,
    bwd_route,
    fwd_gate,
    bwd_gate,
    gain,
    w_in,
    w_out,
):
    meta = jnp.concatenate(
        [
            fwd_route[0].T.astype(F32),
            bwd_route[0].T.astype(F32),
            fwd_gate[0].T,
            bwd_gate[0].T,
        ],
        axis=0,
    )
    pre = jnp.transpose(bwd_pre[0], (1, 0, 2)).reshape(2 * TOK, 2 * FF)
    anywhere = pl.BlockSpec(memory_space=pl.ANY)
    vmem = pl.BlockSpec(memory_space=pltpu.VMEM)
    dma = pltpu.SemaphoreType.DMA

    def buf(*shape):
        return pltpu.VMEM(shape, BF16)

    fwd_out, bwd_out, local_gain, _, _ = pl.pallas_call(
        kernel,
        out_shape=(
            jax.ShapeDtypeStruct((TOK, D), BF16),
            jax.ShapeDtypeStruct((TOK, D), BF16),
            jax.ShapeDtypeStruct((1, D), F32),
            jax.ShapeDtypeStruct((2 * ROWS, D), BF16),
            jax.ShapeDtypeStruct((2 * ROWS, D), BF16),
        ),
        in_specs=[vmem, vmem] + [anywhere] * 6,
        out_specs=(anywhere, anywhere, vmem, anywhere, anywhere),
        scratch_shapes=[
            buf(SLICE, 2 * FF),
            buf(FF, SLICE),
            buf(2 * TOK, D),
            buf(2 * TOK, D),
            buf(4, 2 * ROWS, SLICE),
            buf(4, 2 * ROWS, SLICE),
            buf(4, 2 * ROWS, SLICE),
            buf(4, 2 * ROWS, SLICE),
            buf(4, 2 * ROWS, 2 * FF),
            buf(4, ROWS, 2 * FF),
            buf(4, ROWS, FF),
            buf(2, ROWS, 2 * FF),
            buf(2, ROWS, FF),
            buf(4, 2 * ROWS, FF),
            buf(4, 2 * ROWS, 2 * FF),
            buf(TOK, D),
            buf(TOK, D),
            buf(2 * TOK, 2 * FF),
            buf(4, 80, 2 * FF),
            buf(2, 2, 80, 2 * FF),
            buf(2, 2 * ROWS, SLICE),
            pltpu.VMEM((8, TOK), F32),
            pltpu.VMEM((TOK, 128), F32),
            pltpu.VMEM((2 * TOK, 128), F32),
            buf(2, ROWS, 2 * TOK),
            buf(2, ROWS, 2 * TOK),
            buf(80, 2 * TOK),
            buf(4 * TOK, 2 * ROWS),
            buf(4 * TOK, 2 * ROWS),
            dma((8,)),
            dma((2,)),
            dma((2, 4)),
            dma((4,)),
            dma((4,)),
            dma((2, 2)),
            dma((2, 2)),
            dma((2, 4, 2)),
            dma((2, 4, 2)),
            dma((2, 4, 2)),
            dma((2, 4, 2)),
            dma((2, 4)),
            dma((2, 4)),
            dma((2, 2)),
            dma((2, 2)),
            dma((2, 2)),
            dma((2, 2)),
            dma((2, 4)),
            dma((2, 4)),
            dma((2, 4, 2)),
            dma((2, 4, 2)),
            dma((2, 4)),
            dma((2, 4)),
        ],
        compiler_params=pltpu.CompilerParams(
            collective_id=0, has_side_effects=True, vmem_limit_bytes=64 * 2**20 - 2**16
        ),
        cost_estimate=pl.CostEstimate(
            flops=26 * 10**9, bytes_accessed=40 * 10**6, transcendentals=10**6
        ),
        name="experts",
    )(meta, gain, fwd_sent[0], bwd_sent[0], bwd_saved[0], pre, w_in[0], w_out[0])
    section_gain = lax.psum(local_gain, "ep")
    mirrored = lax.ppermute(section_gain, "pp", [(i, 7 - i) for i in range(8)])
    return (fwd_out[None], bwd_out[None], section_gain + mirrored)


def solution(mesh):
    placed = (
        P("pp", "ep", None),
        P("pp", "ep", None),
        P("pp", "ep", None),
        P("pp", "ep", None, None),
        P("pp", "ep", None),
        P("pp", "ep", None),
        P("pp", "ep", None),
        P("pp", "ep", None),
        P("pp", None),
        P("pp", "ep", None),
        P("pp", None, "ep"),
    )
    return jax.shard_map(
        on_device,
        mesh=mesh,
        in_specs=placed,
        out_specs=(P("pp", "ep", None), P("pp", "ep", None), P("pp", None)),
        check_vma=False,
    )
```

time: 906 us -> 488 us (0.54)
  Pallas kernels: 0 us -> 401 us
  waiting for transfers between devices: 367 us -> 4.77 us
  local copies, waits for them, and re-layouts: 206 us -> 6.8 us
  blocking collectives: 177 us -> 65 us
  other arithmetic: 62.5 us -> 1.25 us
  starting transfers between devices: 41.2 us -> 0.01 us
  matrix products: 38.8 us -> 0 us
    pallas_call x0 -> x1, Pallas kernels: none -> 401 us  [on_device(): pl.pallas_call(kernel, out_shape=(jax.ShapeDtypeStruct((TOK, D), BF16), j...]
    ppermute x9 -> x1, waiting for transfers between devices: 268 us -> 4.77 us  [on_device(): mirrored = lax.ppermute(section_gain, 'pp', [(i, 7 - i) for i in range(8)])]
    all_to_all x4 -> x0, waiting for transfers between devices: 98.5 us -> none  [the longest x1 51.6 us: on_device(): lax.all_to_all(send_grad, 'ep', split_axis=0, concat_axis=0, tiled=True)]
    all_to_all x1 -> x0, blocking collectives: 60.8 us -> none  [on_device(): lax.all_to_all(send_rows, 'ep', split_axis=0, concat_axis=0, tiled=True)]
    gather x5 -> x0, local copies, waits for them, and re-layouts: 55.1 us -> none  [the longest x3 33.4 us: outbound(): return padded[inverse]]
    reshape x8 -> x0, local copies, waits for them, and re-layouts: 53.4 us -> none  [the longest x4 24.3 us: split_send(): rows.reshape(EXPERTS, CAP, slices, piece_width).transpose(0, 2, 1, 3)]
    psum x1, blocking collectives: 117 us -> 65 us  [on_device(): section_gain = lax.psum(local_gain, 'ep')]
    dot_general x4 -> x0, matrix products: 38.8 us -> none  [the longest x1 15.1 us: on_device(): lax.dot_general(jnp.stack([bwd_sum * up_pre * slope, bwd_sum * gate_pre *...]
  transfers between devices with their start and end apart: 13 -> 1, of which waited for: 10 -> 1; matrix products, arithmetic and copies ran while one was open for 6% -> 0% of each run, Pallas kernels for 0% -> 0%
where the time goes in v1:
time: 488 us; the launch traced here: 479 us
  Pallas kernels  401 us (82%)
  blocking collectives  65 us (13%)
  local copies, waits for them, and re-layouts  6.8 us (1%)
    pallas_call x1, Pallas kernels, on_device(): pl.pallas_call(kernel, out_shape=(jax.ShapeDtypeStruct((TOK, D), BF16), j...  401 us
    psum x1, blocking collectives, on_device(): section_gain = lax.psum(local_gain, 'ep')  65 us
  transfers between devices with their start and end apart: 1, of which 1 were waited for; matrix products, arithmetic and copies ran while one was open for 0% of the time, Pallas kernels for 0%

profile of v1, /device:TPU:16, one launch (start us, length us, event | category | flops | bytes accessed | tf_op | source)
XLA Modules:
  0.0 479.1 jit_solution(554000649108288885)
XLA Ops:
  0.6 0.0 copy-start.1
  0.6 0.0 copy-start.2
  0.7 0.0 copy-start.3
  0.7 0.0 copy-start.4
  0.7 2.6 copy.14
  3.2 0.0 copy-done.1
  3.2 0.0 copy-done.2
  3.3 0.0 copy-done.3
  3.3 0.0 copy-done.4
  3.3 0.6 pad_maximum_fusion.meta
  3.9 400.6 %experts.1 = (bf16[128,7168]{1,0:T(8,128)(2,1)}, bf16[128,7168]{1,0:T(8,128)(2,1)}, f32[1,7168]{1,0:T(1,128)}, bf16[288,7168]{1,0:T(8,128)(2,1)}, bf16[288,7168]{1,0:T(8,128)(2,1)}) custom-call(f32[8,128]{1,0:T(8,128)} %pad_maximum_fusion.meta, f32[1,7168]{1,0:T(1,128)} %gain.1, bf16[128,7168]{1,0:T(8,128)(2,1)} %bitcast.33, bf16[128,7168]{1,0:T(8,128)(2,1)} %bitcast.34, ...), custom_call_target="tpu_custom_call" | custom-call | flops 25999998976 | bytes 40000000 | tf_op jit(solution)/shard_map/experts/pallas_call | solution.py:672
  404.5 65.0 %psum.7 = f32[1,7168]{1,0:T(1,128)S(1)} all-reduce(f32[1,7168]{1,0:T(1,128)} %get-tuple-element.8), channel_id=1, replica_groups=mesh['pp'=8,'ep'=16] {'ep'}, use_global_device_ids=true, to_apply=%region_0.0 | all-reduce | flops 7168 | bytes 57344 | tf_op jit(solution)/shard_map/psum | solution.py:745
  469.5 0.0 collective-permute-start
  469.5 4.8 collective-permute-done
  474.3 0.6 add.5
  474.9 0.0 copy-start
  474.9 3.0 copy.17
  477.9 0.0 copy-done
  477.9 1.2 copy.18
  (1 shorter events, 0.0 us)
Async XLA Ops:
  0.6 2.6 copy-start.1
  0.6 2.6 copy-start.2
  0.7 2.6 copy-start.3
  0.7 2.6 copy-start.4
  469.5 4.8 collective-permute-start
  474.9 3.0 copy-start

commit v2 on v1

v2 whole, which is shorter than its diff:
```python
import jax
import jax.numpy as jnp
from jax import lax
from jax.experimental import pallas as pl
from jax.experimental.pallas import tpu as pltpu
from jax.sharding import PartitionSpec as P

D = 7168
FF = 1024
CAP = 72
TOK = 128
SLICE = 1792
PART = 896
ROWS = 2 * CAP
TILE = 256
EPS = 1e-06
F32 = jnp.float32
BF16 = jnp.bfloat16
MESH = pl.DeviceIdType.MESH


def kernel(
    meta,
    gain,
    fwd_sent,
    bwd_sent,
    saved,
    pre,
    w_in,
    w_out,
    fwd_out,
    bwd_out,
    gain_grad,
    ret_f,
    ret_b,
    local_gain,
    w1,
    w2,
    v_f,
    v_b,
    x_f,
    x_b,
    s_f,
    s_b,
    part,
    r1_f,
    r1_b,
    r2_f,
    r2_b,
    h_f,
    h_b,
    xr_f,
    xr_b,
    pre_in,
    pre_out,
    pre_got,
    stage,
    meta_got,
    inv_out,
    inv_got,
    pick_f,
    pick_b,
    pick_pre,
    comb_f,
    comb_b,
    load_sem,
    stage_sem,
    out_sem,
    misc_send,
    misc_recv,
    pre_send,
    pre_recv,
    relay,
    near_send,
    far_send,
    relay_send,
    relay_recv,
    s1_recv,
    gain_got,
    gain_sum,
    gain_send,
    gain_recv,
    d_send,
    d_recv,
    r1_send,
    r1_recv,
    r2_send,
    r2_recv,
    ag_send,
    ag_recv,
    ac_send,
    ac_recv,
    ret_send,
    ret_recv,
    x_send,
    x_recv,
):
    p = lax.axis_index("pp")
    ep = lax.axis_index("ep")
    xh = ep // 8
    z = (ep // 2) % 4
    c = ep % 2
    zp = z % 2
    own_row = pl.multiple_of(xh * TOK, TOK)
    other_row = pl.multiple_of((1 - xh) * TOK, TOK)

    def place(section, dx, dz, dc):
        x2 = (xh + dx) % 2
        z2 = (z + dz) % 4
        c2 = (c + dc) % 2
        return {"pp": section, "ep": x2 * 8 + z2 * 2 + c2}

    def remote(src, dst, send, recv, target):
        return pltpu.make_async_remote_copy(
            src_ref=src,
            dst_ref=dst,
            send_sem=send,
            recv_sem=recv,
            device_id=target,
            device_id_type=MESH,
        )

    def columns(dz, dc):
        j = 2 * ((z + dz) % 2) + (c + dc) % 2
        return pl.multiple_of(j * SLICE, TILE)

    pairs = [(1, 0), (1, 1), (0, 1), (0, 0)]
    even = p % 2 == 0
    near = p + 1 - 2 * (p % 2)
    ahead = (p + 6 + 4 * (p % 2)) % 8

    loads = []
    for q in range(4):
        loads.append(
            pltpu.make_async_copy(
                fwd_sent.at[:, pl.ds(q * SLICE, SLICE)], s_f.at[q, pl.ds(0, TOK)], load_sem.at[q]
            )
        )
    loads.append(pltpu.make_async_copy(pre, pre_in, load_sem.at[4]))
    loads.append(pltpu.make_async_copy(w_in, w1, load_sem.at[5]))
    loads.append(pltpu.make_async_copy(w_out, w2, load_sem.at[6]))
    for load in loads:
        load.start()

    peers = [(near, 0, 0, 0), (near, 1, 0, 0), (7 - p, 0, 0, 0), (7 - p, 1, 0, 0)]
    peers += [((p + 2) % 8, 0, 0, 0), ((p + 6) % 8, 0, 0, 0), (p, 1, 0, 0), (p, 1, 2, 0)]
    far = (p + 7 + 2 * (p % 2)) % 8
    peers += [(far, 0, 0, 0), (far, 1, 0, 0)]
    peers += [(p, 0, dz, dc) for dz in range(4) for dc in range(2) if (dz, dc) != (0, 0)]
    barrier = pltpu.get_barrier_semaphore()
    for peer in peers:
        pl.semaphore_signal(barrier, inc=1, device_id=place(*peer), device_id_type=MESH)
    pl.semaphore_wait(barrier, len(peers))

    meta_copy = remote(meta, meta_got, misc_send.at[0], misc_recv.at[0], place(p, 1, 0, 0))
    meta_copy.start()

    def block_copies(src, dst, send, recv, dz, dc, stream):
        cols = pl.ds(columns(dz, dc), SLICE)
        jr = 2 * dz + dc
        return [
            remote(
                src.at[:, cols],
                dst.at[pl.ds(own_row, TOK), cols],
                send.at[jr, dx],
                recv.at[stream, jr, dx],
                place(near, dx, 0, 0),
            )
            for dx in range(2)
        ]

    def relay_copy(src, dz, dc):
        cols = pl.ds(columns(dz, dc), SLICE)
        jr = 2 * dz + dc
        return remote(
            src.at[:, cols],
            relay.at[:, cols],
            relay_send.at[jr],
            relay_recv.at[jr],
            place(ahead, 0, 0, 0),
        )

    def start_forward(pair):
        @pl.when(even)
        def _():
            for copy in block_copies(fwd_sent, v_f, near_send, s1_recv, *pair, 0):
                copy.start()

        @pl.when(jnp.logical_not(even))
        def _():
            relay_copy(fwd_sent, *pair).start()

    def relay_forward(pair):
        @pl.when(jnp.logical_not(even))
        def _():
            relay_copy(fwd_sent, *pair).wait_recv()
            for copy in block_copies(relay, v_f, far_send, s1_recv, *pair, 0):
                copy.start()

    def start_backward(pair):
        @pl.when(even)
        def _():
            relay_copy(bwd_sent, *pair).start()

    def relay_backward(pair):
        @pl.when(even)
        def _():
            relay_copy(bwd_sent, *pair).wait_recv()
            for copy in block_copies(relay, v_b, far_send, s1_recv, *pair, 1):
                copy.start()

        @pl.when(jnp.logical_not(even))
        def _():
            for copy in block_copies(bwd_sent, v_b, near_send, s1_recv, *pair, 1):
                copy.start()

    def arrived(stream, v, pair):
        for copy in block_copies(fwd_sent, v, near_send, s1_recv, *pair, stream):
            copy.wait_recv()

    for pair in pairs[:2]:
        start_forward(pair)
    for pair in pairs:
        start_backward(pair)

    total = jnp.zeros((TOK, 1), F32)
    for q in range(4):
        loads[q].wait()
        block = s_f[q, pl.ds(0, TOK), :].astype(F32)
        total = total + jnp.sum(block * block, axis=1, keepdims=True)
    inv_out[...] = jnp.broadcast_to(lax.rsqrt(total / D + EPS), (TOK, 128))
    inv_copies = [
        remote(
            inv_out,
            inv_got.at[pl.ds(own_row, TOK)],
            misc_send.at[1 + dx],
            misc_recv.at[1 + dx],
            place((p + 1) % 8, dx, 0, 0),
        )
        for dx in range(2)
    ]
    for copy in inv_copies:
        copy.start()

    meta_copy.wait_recv()
    own_meta = meta[...]
    got_meta = meta_got[...]
    row_id = lax.broadcasted_iota(jnp.int32, (TOK, TOK), 0)
    col_id = lax.broadcasted_iota(jnp.int32, (TOK, TOK), 1)
    before = jnp.where(row_id < col_id, 1.0, 0.0).astype(BF16)

    def slots(block, stream, expert):
        expert = expert.astype(F32)
        hit0 = jnp.where(block[2 * stream : 2 * stream + 1] == expert, 1.0, 0.0)
        hit1 = jnp.where(block[2 * stream + 1 : 2 * stream + 2] == expert, 1.0, 0.0)
        hit = hit0 + hit1
        wide = jnp.broadcast_to(hit, (16, TOK)).astype(BF16)
        slot = jnp.dot(wide, before, preferred_element_type=F32)[0:1]
        gate = (
            block[4 + 2 * stream : 5 + 2 * stream] * hit0
            + block[5 + 2 * stream : 6 + 2 * stream] * hit1
        )
        return hit0, hit1, hit, slot, gate

    for stream, pick, comb in ((0, pick_f, comb_f), (1, pick_b, comb_b)):
        rows_needed = []
        for local in range(2):
            expert = 2 * xh + local
            own = slots(own_meta, stream, expert)
            got = slots(got_meta, stream, expert)
            low = xh == 0
            hit_row = jnp.concatenate(
                [jnp.where(low, own[2], got[2]), jnp.where(low, got[2], own[2])], axis=1
            )
            slot_row = jnp.concatenate(
                [jnp.where(low, own[3], got[3]), jnp.where(low, got[3], own[3]) + CAP], axis=1
            )
            line = lax.broadcasted_iota(jnp.int32, (ROWS, 2 * TOK), 0).astype(F32)
            pick[local] = jnp.where((line == slot_row) & (hit_row > 0.5), 1.0, 0.0).astype(BF16)
            for side in (own, got):
                rows_needed += [side[3], side[4]]
        padding = jnp.zeros((TOK - len(rows_needed), TOK), F32)
        turned = jnp.concatenate(rows_needed + [padding], axis=0).T
        lane = lax.broadcasted_iota(jnp.int32, (TOK, 2 * ROWS), 1).astype(F32)
        for side in range(2):
            home = jnp.where(xh == 0, side, 1 - side).astype(F32)
            mix = jnp.zeros((TOK, 2 * ROWS), F32)
            for local in range(2):
                k = 2 * (2 * local + side)
                slot_col = turned[:, k : k + 1] + (home * CAP + local * ROWS)
                gate_col = turned[:, k + 1 : k + 2]
                mix = mix + jnp.where(lane == slot_col, gate_col, 0.0)
            high = mix.astype(BF16)
            comb[pl.ds(2 * side * TOK, TOK), :] = high
            comb[pl.ds((2 * side + 1) * TOK, TOK), :] = (mix - high.astype(F32)).astype(BF16)

    loads[4].wait()
    pre_copies = {}
    for dx in range(2):
        for i in range(2):
            expert = 2 * ((xh + dx) % 2) + ((z + 2 * i) % 4) // 2
            hit0, hit1, _, slot, _ = slots(own_meta, 1, expert)
            hit_row = jnp.concatenate([hit0, hit1], axis=1)
            slot_row = jnp.concatenate([slot, slot], axis=1)
            line = lax.broadcasted_iota(jnp.int32, (80, 2 * TOK), 0).astype(F32)
            pick_pre[...] = jnp.where((line == slot_row) & (hit_row > 0.5), 1.0, 0.0).astype(BF16)
            target = pre_got.at[i, xh] if (dx, i) == (0, 0) else pre_out.at[2 * dx + i]

            def gather_pre(t, carry, target=target):
                cols = pl.ds(pl.multiple_of(t * 512, 512), 512)
                target[:, cols] = jnp.dot(
                    pick_pre[...], pre_in[:, cols], preferred_element_type=F32
                ).astype(BF16)
                return carry

            lax.fori_loop(0, 4, gather_pre, 0)
            if (dx, i) != (0, 0):
                copy = remote(
                    pre_out.at[2 * dx + i],
                    pre_got.at[i, xh],
                    pre_send.at[i, dx],
                    pre_recv.at[i, dx],
                    place(p, dx, 2 * i, 0),
                )
                copy.start()
                pre_copies[dx, i] = copy

    rows0, rows1 = pl.ds(0, ROWS), pl.ds(ROWS, ROWS)
    partner = {"pp": p, "ep": xh * 8 + (z + 1 - 2 * zp) * 2 + c}
    fwd = dict(
        v=v_f, x=x_f, s=s_f, h=h_f, r1=r1_f, r2=r2_f, ret=ret_f, xr=xr_f, pick=pick_f, comb=comb_f
    )
    bwd = dict(
        v=v_b, x=x_b, s=s_b, h=h_b, r1=r1_b, r2=r2_b, ret=ret_b, xr=xr_b, pick=pick_b, comb=comb_b
    )
    fwd.update(number=0, width=2 * FF)
    bwd.update(number=1, width=FF)
    for stream in (fwd, bwd):
        for name in ("sent", "core", "chip", "ag", "ac", "back", "over"):
            stream[name] = {}

    def dispatch(stream, dzp, dc):
        number, v, s, x = stream["number"], stream["v"], stream["s"], stream["x"]
        base = columns(dzp, dc)
        targets = []
        for dz in (dzp, dzp + 2):
            here = x if (dz, dc) == (0, 0) else s
            targets.append((here, dz, ((z + dz) % 4) // 2))

        def gather(t, carry):
            cols = pl.ds(pl.multiple_of(base + t * TILE, TILE), TILE)
            block = v[:, cols]
            if number == 0:
                block = (block.astype(F32) * inv_got[:, 0:1] * gain[:, cols]).astype(BF16)
            where = pl.ds(pl.multiple_of(t * TILE, TILE), TILE)
            for ref, dz, local in targets:
                ref[dz, pl.ds(dc * ROWS, ROWS), where] = jnp.dot(
                    stream["pick"][local], block, preferred_element_type=F32
                ).astype(BF16)
            return carry

        lax.fori_loop(0, SLICE // TILE, gather, 0)
        for dz in (dzp + 2, dzp):
            if (dz, dc) == (0, 0):
                continue
            rows = pl.ds(dc * ROWS, ROWS)
            copy = remote(
                s.at[dz, rows],
                x.at[dz, rows],
                d_send.at[number, dz, dc],
                d_recv.at[number, dz, dc],
                place(p, 0, dz, dc),
            )
            copy.start()
            stream["sent"][dz, dc] = copy

    def multiply(lhs, w, out, count, tile, turned):
        def step(t, carry):
            cols = pl.ds(pl.multiple_of(t * tile, tile), tile)
            if turned:
                got = lax.dot_general(
                    lhs[...], w[cols, :], (((1,), (1,)), ((), ())), preferred_element_type=F32
                )
            else:
                got = jnp.dot(lhs[...], w[:, cols], preferred_element_type=F32)
            out[:, cols] = got.astype(BF16)
            return carry

        lax.fori_loop(0, count // tile, step, 0)

    def first_product(stream, dz):
        number, x, width = stream["number"], stream["x"], stream["width"]
        for dc in range(2):
            if (dz, dc) != (0, 0):
                stream["sent"][dz, dc].wait_recv()
        out = part.at[dz, :, pl.ds(0, width)]
        if number == 0:
            multiply(x.at[dz], w1, out, width, 512, False)
        else:
            multiply(x.at[dz], w2, out, width, 512, True)
        copy = remote(
            part.at[dz, rows1, pl.ds(0, width)],
            stream["r1"].at[dz],
            r1_send.at[number, dz],
            r1_recv.at[number, dz],
            place(p, 0, 0, 1),
        )
        copy.start()
        stream["core"][dz] = copy

    def chip_sum(stream, dz):
        number, r1, width = stream["number"], stream["r1"], stream["width"]
        stream["core"][dz].wait_recv()

        def add(t, carry):
            cols = pl.ds(pl.multiple_of(t * 512, 512), 512)
            part[dz, rows0, cols] = (
                part[dz, rows0, cols].astype(F32) + r1[dz, :, cols].astype(F32)
            ).astype(BF16)
            return carry

        lax.fori_loop(0, width // 512, add, 0)
        if dz % 2 == 1:
            index = ((dz + 5 - 2 * zp) % 4) // 2
            copy = remote(
                part.at[dz, rows0, pl.ds(0, width)],
                stream["r2"].at[index],
                r2_send.at[number, dz // 2],
                r2_recv.at[number, index],
                partner,
            )
            copy.start()
            stream["chip"][dz] = copy

    def to_core(stream, dz):
        number, h = stream["number"], stream["h"]
        copy = remote(
            h.at[dz, rows0],
            h.at[dz, rows1],
            ac_send.at[number, dz],
            ac_recv.at[number, dz],
            place(p, 0, 0, 1),
        )
        copy.start()
        stream["ac"][dz] = copy

    def activate(stream, dz):
        number, h, r2, width = stream["number"], stream["h"], stream["r2"], stream["width"]
        i = dz // 2
        remote(
            part.at[0, rows0, pl.ds(0, width)],
            r2.at[i],
            r2_send.at[number, 0],
            r2_recv.at[number, i],
            partner,
        ).wait_recv()
        if number == 1:
            for dx in range(2):
                if (dx, i) != (0, 0):
                    pre_copies[dx, i].wait_recv()

        def step(t, carry):
            lo = pl.ds(pl.multiple_of(t * TILE, TILE), TILE)
            hi = pl.ds(pl.multiple_of(t * TILE + FF, TILE), TILE)
            if number == 0:
                g = part[dz, rows0, lo].astype(F32) + r2[i, :, lo].astype(F32)
                u = part[dz, rows0, hi].astype(F32) + r2[i, :, hi].astype(F32)
                h[dz, rows0, lo] = (g / (1.0 + jnp.exp(-g)) * u).astype(BF16)
            else:
                hg = part[dz, rows0, lo].astype(F32) + r2[i, :, lo].astype(F32)
                g = jnp.concatenate(
                    [pre_got[i, k, :, lo].astype(F32)[0:CAP] for k in range(2)], axis=0
                )
                u = jnp.concatenate(
                    [pre_got[i, k, :, hi].astype(F32)[0:CAP] for k in range(2)], axis=0
                )
                sig = 1.0 / (1.0 + jnp.exp(-g))
                h[dz, rows0, lo] = (hg * u * sig * (1.0 + g * (1.0 - sig))).astype(BF16)
                h[dz, rows0, hi] = (hg * g * sig).astype(BF16)
            return carry

        lax.fori_loop(0, FF // TILE, step, 0)
        there = (dz + 5 - 2 * zp) % 4
        copy = remote(
            h.at[dz, rows0],
            h.at[there, rows0],
            ag_send.at[number, i],
            ag_recv.at[number, there // 2],
            partner,
        )
        copy.start()
        stream["ag"][dz] = copy
        to_core(stream, dz)

    def forward_on(stream, dz):
        number, h = stream["number"], stream["h"]
        i = dz // 2
        remote(
            h.at[dz - 1, rows0],
            h.at[dz, rows0],
            ag_send.at[number, i],
            ag_recv.at[number, i],
            partner,
        ).wait_recv()
        to_core(stream, dz)

    def second_product(stream, dz):
        number, h, s, ret = stream["number"], stream["h"], stream["s"], stream["ret"]
        region = ret.at[
            pl.ds(pl.multiple_of(z // 2 * ROWS, ROWS), ROWS), pl.ds(columns(0, 0), SLICE)
        ]
        stream["ac"][dz].wait_recv()
        for dc in range(2):
            if (dz, dc) != (0, 0):
                stream["sent"][dz, dc].wait_send()
        if number == 0:
            multiply(h.at[dz], w2, s.at[dz], SLICE, TILE, False)
        else:
            multiply(h.at[dz], w1, s.at[dz], SLICE, TILE, True)
        for dc in range(2):
            rows = pl.ds(dc * ROWS, ROWS)
            if (dz, dc) == (0, 0):
                copy = pltpu.make_async_copy(s.at[dz, rows], region, ret_recv.at[number, 0, 0])
            else:
                copy = remote(
                    s.at[dz, rows],
                    region,
                    ret_send.at[number, dz, dc],
                    ret_recv.at[number, dz, dc],
                    place(p, 0, 4 - dz, dc),
                )
            copy.start()
            stream["back"][dz, dc] = copy

    def combine(stream, dzp):
        number, v, x, ret = stream["number"], stream["v"], stream["x"], stream["ret"]
        fetches = []
        for dc in (1, 0):
            for dz in (dzp, dzp + 2):
                if (dz, dc) == (0, 0):
                    stream["back"][dz, dc].wait()
                else:
                    stream["back"][dz, dc].wait_recv()
            fetch = pltpu.make_async_copy(
                ret.at[:, pl.ds(columns(dzp, dc), SLICE)], stage.at[dc], stage_sem.at[dc]
            )
            fetch.start()
            fetches.append(fetch)
        for dc in (1, 0):
            fetches[1 - dc].wait()
            base = columns(dzp, dc)
            jr = 2 * dzp + dc

            def step(t, carry, dc=dc, base=base, jr=jr):
                cols = pl.ds(pl.multiple_of(t * TILE, TILE), TILE)
                mixed = jnp.dot(
                    stream["comb"][...], stage[dc, :, cols], preferred_element_type=F32
                )
                own = mixed[0:TOK] + mixed[TOK : 2 * TOK]
                other = mixed[2 * TOK : 3 * TOK] + mixed[3 * TOK :]
                high = own.astype(BF16)
                x[jr, pl.ds(0, TOK), cols] = high
                x[jr, pl.ds(TOK, TOK), cols] = (own - high.astype(F32)).astype(BF16)
                out_cols = pl.ds(pl.multiple_of(base + t * TILE, TILE), TILE)
                v[pl.ds(other_row, TOK), out_cols] = other.astype(BF16)
                return carry

            lax.fori_loop(0, SLICE // TILE, step, 0)
            copy = remote(
                v.at[pl.ds(other_row, TOK), pl.ds(base, SLICE)],
                stream["xr"].at[:, pl.ds(base, SLICE)],
                x_send.at[number, jr],
                x_recv.at[number, jr],
                place(p, 1, 0, 0),
            )
            copy.start()
            stream["over"][dzp, dc] = copy

    late = [(0, 1), (0, 0), (1, 1), (1, 0)]

    def finish_forward(crossed):
        for dzp, dc in late:
            crossed[dzp, dc].wait_recv()
            base = columns(dzp, dc)
            jr = 2 * dzp + dc

            def step(t, carry, base=base, jr=jr):
                cols = pl.ds(pl.multiple_of(t * TILE, TILE), TILE)
                wide = pl.ds(pl.multiple_of(base + t * TILE, TILE), TILE)
                here = pl.ds(own_row, TOK)
                mine = x_f[jr, pl.ds(0, TOK), cols].astype(F32)
                mine = mine + x_f[jr, pl.ds(TOK, TOK), cols].astype(F32)
                v_f[here, wide] = (
                    v_f[here, wide].astype(F32) + (mine + xr_f[:, wide].astype(F32))
                ).astype(BF16)
                return carry

            lax.fori_loop(0, SLICE // TILE, step, 0)
            copy = pltpu.make_async_copy(
                v_f.at[pl.ds(own_row, TOK), pl.ds(base, SLICE)],
                fwd_out.at[:, pl.ds(base, SLICE)],
                out_sem.at[0, jr],
            )
            copy.start()
            outs.append(copy)

    def finish_backward(crossed):
        total = jnp.zeros((TOK, 1), F32)
        for n, (dzp, dc) in enumerate(late):
            saved_loads[n].wait()
            block = s_f[2 * dzp + dc, pl.ds(0, TOK), :].astype(F32)
            total = total + jnp.sum(block * block, axis=1, keepdims=True)
        inv = lax.rsqrt(total / D + EPS)
        dots = jnp.zeros((TOK, TILE), F32)
        for dzp, dc in late:
            crossed[dzp, dc].wait_recv()
            base = columns(dzp, dc)
            jr = 2 * dzp + dc

            def step(t, carry, base=base, jr=jr):
                cols = pl.ds(pl.multiple_of(t * TILE, TILE), TILE)
                wide = pl.ds(pl.multiple_of(base + t * TILE, TILE), TILE)
                grad = x_b[jr, pl.ds(0, TOK), cols].astype(F32)
                grad = grad + x_b[jr, pl.ds(TOK, TOK), cols].astype(F32)
                grad = grad + xr_b[:, wide].astype(F32)
                high = grad.astype(BF16)
                x_b[jr, pl.ds(0, TOK), cols] = high
                x_b[jr, pl.ds(TOK, TOK), cols] = (grad - high.astype(F32)).astype(BF16)
                w = s_f[jr, pl.ds(0, TOK), cols].astype(F32)
                local_gain[:, wide] = jnp.sum(grad * w * inv, axis=0, keepdims=True)
                return carry + w * gain[:, wide] * grad

            dots = lax.fori_loop(0, SLICE // TILE, step, dots)
        scale = inv * inv * inv * (jnp.sum(dots, axis=1, keepdims=True) / D)
        waiting = gain_cores()
        for n, (dzp, dc) in enumerate(late):
            if n == 1:
                waiting = gain_sides(waiting)
            if n == 2:
                waiting = gain_spread(waiting)
            base = columns(dzp, dc)
            jr = 2 * dzp + dc

            def last(t, carry, base=base, jr=jr):
                cols = pl.ds(pl.multiple_of(t * TILE, TILE), TILE)
                wide = pl.ds(pl.multiple_of(base + t * TILE, TILE), TILE)
                here = pl.ds(own_row, TOK)
                grad = x_b[jr, pl.ds(0, TOK), cols].astype(F32)
                grad = grad + x_b[jr, pl.ds(TOK, TOK), cols].astype(F32)
                w = s_f[jr, pl.ds(0, TOK), cols].astype(F32)
                v_b[here, wide] = (
                    v_b[here, wide].astype(F32) + inv * (gain[:, wide] * grad) - w * scale
                ).astype(BF16)
                return carry

            lax.fori_loop(0, SLICE // TILE, last, 0)
            copy = pltpu.make_async_copy(
                v_b.at[pl.ds(own_row, TOK), pl.ds(base, SLICE)],
                bwd_out.at[:, pl.ds(base, SLICE)],
                out_sem.at[1, jr],
            )
            copy.start()
            outs.append(copy)
        for copy in waiting:
            copy.wait_recv()

    half = pl.multiple_of(c * 4 * PART, 128)
    half_other = pl.multiple_of((1 - c) * 4 * PART, 128)
    gain_copies = []

    def send_gain(src, dst, index, target):
        copy = remote(src, dst, gain_send.at[index], gain_recv.at[index], target)
        copy.start()
        gain_copies.append(copy)
        return copy

    def piece(dz):
        return pl.ds(pl.multiple_of(half + (z + dz) % 4 * PART, 128), PART)

    def gain_cores():
        size = pl.ds(half_other, 4 * PART)
        copy = send_gain(local_gain.at[:, size], gain_got.at[:, size], 0, place(p, 0, 0, 1))
        copy.wait_recv()
        size = pl.ds(half, 4 * PART)
        local_gain[:, size] = local_gain[:, size] + gain_got[:, size]
        return [
            send_gain(
                local_gain.at[:, piece(dz)], gain_sum.at[pl.ds(dz, 1)], dz, place(p, 0, dz, 0)
            )
            for dz in range(1, 4)
        ]

    def gain_sides(copies):
        for copy in copies:
            copy.wait_recv()
        mine = local_gain[:, piece(0)]
        for dz in range(1, 4):
            mine = mine + gain_sum[pl.ds(dz, 1)]
        gain_sum[0:1] = mine
        targets = [place(p, 1, 0, 0), place(7 - p, 0, 0, 0), place(7 - p, 1, 0, 0)]
        return [
            send_gain(gain_sum.at[pl.ds(0, 1)], gain_sum.at[pl.ds(4 + i, 1)], 4 + i, target)
            for i, target in enumerate(targets)
        ]

    def gain_spread(copies):
        for copy in copies:
            copy.wait_recv()
        here = gain_sum[0:1] + gain_sum[4:5]
        gain_grad[:, piece(0)] = here + (gain_sum[5:6] + gain_sum[6:7])
        return [
            send_gain(
                gain_grad.at[:, piece(0)],
                gain_grad.at[:, piece(0)],
                8 + 2 * dz + dc,
                place(p, 0, dz, dc),
            )
            for dz in range(4)
            for dc in range(2)
            if (dz, dc) != (0, 0)
        ]

    def sends_done(copies):
        for copy in copies:
            copy.wait_send()

    outs = []
    for copy in inv_copies:
        copy.wait_recv()

    def dispatch_forward(n):
        relay_forward(pairs[n])
        arrived(0, v_f, pairs[n])
        if n + 2 < 4:
            start_forward(pairs[n + 2])
        else:
            relay_backward(pairs[n - 2])
        dispatch(fwd, *pairs[n])

    def dispatch_backward(n):
        arrived(1, v_b, pairs[n])
        dispatch(bwd, *pairs[n])

    def first_product_again(dz):
        fwd["core"][dz].wait_send()
        if dz % 2 == 1:
            fwd["chip"][dz].wait_send()
        first_product(bwd, dz)

    dispatch_forward(0)
    dispatch_forward(1)
    dispatch_forward(2)
    loads[5].wait()
    first_product(fwd, 1)
    first_product(fwd, 3)
    dispatch_forward(3)
    chip_sum(fwd, 1)
    chip_sum(fwd, 3)
    relay_backward(pairs[2])
    relay_backward(pairs[3])
    first_product(fwd, 0)
    first_product(fwd, 2)
    chip_sum(fwd, 0)
    chip_sum(fwd, 2)
    loads[6].wait()
    dispatch_backward(0)
    dispatch_backward(1)
    activate(fwd, 0)
    activate(fwd, 2)
    dispatch_backward(2)
    second_product(fwd, 0)
    second_product(fwd, 2)
    first_product_again(1)
    first_product_again(3)
    forward_on(fwd, 1)
    forward_on(fwd, 3)
    dispatch_backward(3)
    second_product(fwd, 1)
    second_product(fwd, 3)
    chip_sum(bwd, 1)
    chip_sum(bwd, 3)
    first_product_again(0)
    first_product_again(2)
    chip_sum(bwd, 0)
    chip_sum(bwd, 2)
    combine(fwd, 0)
    activate(bwd, 0)
    activate(bwd, 2)
    combine(fwd, 1)
    second_product(bwd, 0)
    second_product(bwd, 2)
    forward_on(bwd, 1)
    forward_on(bwd, 3)
    second_product(bwd, 1)
    second_product(bwd, 3)
    sends_done([copy for key, copy in fwd["back"].items() if key != (0, 0)])
    saved_loads = []
    for n, (dzp, dc) in enumerate(late):
        copy = pltpu.make_async_copy(
            saved.at[:, pl.ds(columns(dzp, dc), SLICE)],
            s_f.at[2 * dzp + dc, pl.ds(0, TOK)],
            load_sem.at[n],
        )
        copy.start()
        saved_loads.append(copy)
    combine(bwd, 0)
    combine(bwd, 1)
    finish_forward(fwd["over"])
    finish_backward(bwd["over"])

    sends_done([meta_copy] + inv_copies + list(pre_copies.values()) + gain_copies)
    for pair in pairs:
        relay_copy(fwd_sent, *pair).wait_send()
        for copy in block_copies(fwd_sent, v_f, near_send, s1_recv, *pair, 0):
            copy.wait_send()
        for copy in block_copies(relay, v_f, far_send, s1_recv, *pair, 0):
            copy.wait_send()
    for stream in (fwd, bwd):
        for name in ("ag", "ac", "over"):
            sends_done(stream[name].values())
    for name in ("core", "chip"):
        sends_done(bwd[name].values())
    sends_done([copy for key, copy in bwd["back"].items() if key != (0, 0)])
    for copy in outs:
        copy.wait()


def on_device(
    fwd_sent,
    bwd_sent,
    bwd_saved,
    bwd_pre,
    fwd_route,
    bwd_route,
    fwd_gate,
    bwd_gate,
    gain,
    w_in,
    w_out,
):
    meta = jnp.concatenate(
        [
            fwd_route[0].T.astype(F32),
            bwd_route[0].T.astype(F32),
            fwd_gate[0].T,
            bwd_gate[0].T,
        ],
        axis=0,
    )
    pre = jnp.transpose(bwd_pre[0], (1, 0, 2)).reshape(2 * TOK, 2 * FF)
    anywhere = pl.BlockSpec(memory_space=pl.ANY)
    vmem = pl.BlockSpec(memory_space=pltpu.VMEM)
    dma = pltpu.SemaphoreType.DMA

    def buf(*shape):
        return pltpu.VMEM(shape, BF16)

    fwd_out, bwd_out, gain_grad, _, _ = pl.pallas_call(
        kernel,
        out_shape=(
            jax.ShapeDtypeStruct((TOK, D), BF16),
            jax.ShapeDtypeStruct((TOK, D), BF16),
            jax.ShapeDtypeStruct((1, D), F32),
            jax.ShapeDtypeStruct((2 * ROWS, D), BF16),
            jax.ShapeDtypeStruct((2 * ROWS, D), BF16),
        ),
        in_specs=[vmem, vmem] + [anywhere] * 6,
        out_specs=(anywhere, anywhere, vmem, anywhere, anywhere),
        scratch_shapes=[
            pltpu.VMEM((1, D), F32),
            buf(SLICE, 2 * FF),
            buf(FF, SLICE),
            buf(2 * TOK, D),
            buf(2 * TOK, D),
            buf(4, 2 * ROWS, SLICE),
            buf(4, 2 * ROWS, SLICE),
            buf(4, 2 * ROWS, SLICE),
            buf(4, 2 * ROWS, SLICE),
            buf(4, 2 * ROWS, 2 * FF),
            buf(4, ROWS, 2 * FF),
            buf(4, ROWS, FF),
            buf(2, ROWS, 2 * FF),
            buf(2, ROWS, FF),
            buf(4, 2 * ROWS, FF),
            buf(4, 2 * ROWS, 2 * FF),
            buf(TOK, D),
            buf(TOK, D),
            buf(2 * TOK, 2 * FF),
            buf(4, 80, 2 * FF),
            buf(2, 2, 80, 2 * FF),
            buf(2, 2 * ROWS, SLICE),
            pltpu.VMEM((8, TOK), F32),
            pltpu.VMEM((TOK, 128), F32),
            pltpu.VMEM((2 * TOK, 128), F32),
            buf(2, ROWS, 2 * TOK),
            buf(2, ROWS, 2 * TOK),
            buf(80, 2 * TOK),
            buf(4 * TOK, 2 * ROWS),
            buf(4 * TOK, 2 * ROWS),
            dma((8,)),
            dma((2,)),
            dma((2, 4)),
            dma((4,)),
            dma((4,)),
            dma((2, 2)),
            dma((2, 2)),
            buf(TOK, D),
            dma((4, 2)),
            dma((4, 2)),
            dma((4,)),
            dma((4,)),
            dma((2, 4, 2)),
            pltpu.VMEM((1, D), F32),
            pltpu.VMEM((8, PART), F32),
            dma((16,)),
            dma((16,)),
            dma((2, 4, 2)),
            dma((2, 4, 2)),
            dma((2, 4)),
            dma((2, 4)),
            dma((2, 2)),
            dma((2, 2)),
            dma((2, 2)),
            dma((2, 2)),
            dma((2, 4)),
            dma((2, 4)),
            dma((2, 4, 2)),
            dma((2, 4, 2)),
            dma((2, 4)),
            dma((2, 4)),
        ],
        compiler_params=pltpu.CompilerParams(
            collective_id=0, has_side_effects=True, vmem_limit_bytes=64 * 2**20 - 2**16
        ),
        cost_estimate=pl.CostEstimate(
            flops=26 * 10**9, bytes_accessed=40 * 10**6, transcendentals=10**6
        ),
        name="experts",
    )(meta, gain, fwd_sent[0], bwd_sent[0], bwd_saved[0], pre, w_in[0], w_out[0])
    return (fwd_out[None], bwd_out[None], gain_grad)


def solution(mesh):
    placed = (
        P("pp", "ep", None),
        P("pp", "ep", None),
        P("pp", "ep", None),
        P("pp", "ep", None, None),
        P("pp", "ep", None),
        P("pp", "ep", None),
        P("pp", "ep", None),
        P("pp", "ep", None),
        P("pp", None),
        P("pp", "ep", None),
        P("pp", None, "ep"),
    )
    return jax.shard_map(
        on_device,
        mesh=mesh,
        in_specs=placed,
        out_specs=(P("pp", "ep", None), P("pp", "ep", None), P("pp", None)),
        check_vma=False,
    )
```

time: 488 us -> 372 us (0.76); the launches traced: 479 us -> 369 us
  blocking collectives: 65 us -> 0 us
  Pallas kernels: 401 us -> 359 us
    psum x1 -> x0, blocking collectives: 65 us -> none  [on_device(): section_gain = lax.psum(local_gain, 'ep')]
    pallas_call x1, Pallas kernels: 401 us -> 359 us  [on_device(): pl.pallas_call(kernel, out_shape=(jax.ShapeDtypeStruct((TOK, D), BF16), j...]
  transfers between devices with their start and end apart: 1 -> 0, of which waited for: 1 -> 0; matrix products, arithmetic and copies ran while one was open for 0% -> 0% of each run, Pallas kernels for 0% -> 0%
where the time goes in v2:
time: 372 us; the launch traced here: 369 us
  Pallas kernels  359 us (97%)
  local copies, waits for them, and re-layouts  7.37 us (2%)
    pallas_call x1, Pallas kernels, on_device(): pl.pallas_call(kernel, out_shape=(jax.ShapeDtypeStruct((TOK, D), BF16), j...  359 us

profile of v2, /device:TPU:16, one launch (start us, length us, event | category | flops | bytes accessed | tf_op | source)
XLA Modules:
  0.0 369.5 jit_solution(1332932090231745366)
XLA Ops:
  0.6 0.7 convert_bitcast_fusion
  1.3 1.3 pad_maximum_fusion.meta
  2.6 2.5 copy.14
  5.2 359.5 %experts.1 = (bf16[128,7168]{1,0:T(8,128)(2,1)}, bf16[128,7168]{1,0:T(8,128)(2,1)}, f32[1,7168]{1,0:T(1,128)}, bf16[288,7168]{1,0:T(8,128)(2,1)}, bf16[288,7168]{1,0:T(8,128)(2,1)}) custom-call(f32[8,128]{1,0:T(8,128)} %pad_maximum_fusion.meta, f32[1,7168]{1,0:T(1,128)} %gain.1, bf16[128,7168]{1,0:T(8,128)(2,1)} %bitcast.33, bf16[128,7168]{1,0:T(8,128)(2,1)} %bitcast.34, ...), custom_call_target="tpu_custom_call" | custom-call | flops 25999998976 | bytes 40000000 | tf_op jit(solution)/shard_map/experts/pallas_call | solution.py:858
  364.6 0.0 copy-start
  364.6 3.0 copy.18
  367.6 0.0 copy-done
  367.6 0.0 copy-start.1
  367.6 1.2 copy.19
  368.9 0.0 copy-done.1
  368.9 0.6 copy.20
Async XLA Ops:
  364.6 3.0 copy-start
  367.6 1.2 copy-start.1

commit v3 on v2

--- a/solution.py
+++ b/solution.py
@@ -14,6 +14,8 @@
 ROWS = 2 * CAP
 TILE = 256
 EPS = 1e-06
+HALVES = ((0, 768), (768, 1024))
+PIECES = ((0, 512), (512, 512), (1024, 512), (1536, 256))
 F32 = jnp.float32
 BF16 = jnp.bfloat16
 MESH = pl.DeviceIdType.MESH
@@ -124,7 +126,10 @@
         j = 2 * ((z + dz) % 2) + (c + dc) % 2
         return pl.multiple_of(j * SLICE, TILE)
 
-    pairs = [(1, 0), (1, 1), (0, 1), (0, 0)]
+    pairs = [(dz, dc, k) for dz, dc in ((0, 1), (0, 0), (1, 0), (1, 1)) for k in range(2)]
+    near_z = 1 + 2 * zp
+    far_z = 3 - 2 * zp
+    mirror = 7 - 2 * z
     even = p % 2 == 0
     near = p + 1 - 2 * (p % 2)
     ahead = (p + 6 + 4 * (p % 2)) % 8
@@ -143,7 +148,7 @@
         load.start()
 
     peers = [(near, 0, 0, 0), (near, 1, 0, 0), (7 - p, 0, 0, 0), (7 - p, 1, 0, 0)]
-    peers += [((p + 2) % 8, 0, 0, 0), ((p + 6) % 8, 0, 0, 0), (p, 1, 0, 0), (p, 1, 2, 0)]
+    peers += [((p + 2) % 8, 0, 0, 0), ((p + 6) % 8, 0, 0, 0), (p, 1, 0, 0), (p, 1, mirror, 0)]
     far = (p + 7 + 2 * (p % 2)) % 8
     peers += [(far, 0, 0, 0), (far, 1, 0, 0)]
     peers += [(p, 0, dz, dc) for dz in range(4) for dc in range(2) if (dz, dc) != (0, 0)]
@@ -155,9 +160,13 @@
     meta_copy = remote(meta, meta_got, misc_send.at[0], misc_recv.at[0], place(p, 1, 0, 0))
     meta_copy.start()
 
-    def block_copies(src, dst, send, recv, dz, dc, stream):
-        cols = pl.ds(columns(dz, dc), SLICE)
-        jr = 2 * dz + dc
+    def half_columns(dz, dc, k):
+        begin, size = HALVES[k]
+        return pl.ds(pl.multiple_of(columns(dz, dc) + begin, TILE), size)
+
+    def block_copies(src, dst, send, recv, dz, dc, k, stream):
+        cols = half_columns(dz, dc, k)
+        jr = 4 * dz + 2 * dc + k
         return [
             remote(
                 src.at[:, cols],
@@ -169,9 +178,9 @@
             for dx in range(2)
         ]
 
-    def relay_copy(src, dz, dc):
-        cols = pl.ds(columns(dz, dc), SLICE)
-        jr = 2 * dz + dc
+    def relay_copy(src, dz, dc, k):
+        cols = half_columns(dz, dc, k)
+        jr = 4 * dz + 2 * dc + k
         return remote(
             src.at[:, cols],
             relay.at[:, cols],
@@ -220,8 +229,56 @@
 
     for pair in pairs[:2]:
         start_forward(pair)
-    for pair in pairs:
-        start_backward(pair)
+
+    own_meta = meta[...]
+    row_id = lax.broadcasted_iota(jnp.int32, (TOK, TOK), 0)
+    col_id = lax.broadcasted_iota(jnp.int32, (TOK, TOK), 1)
+    before = jnp.where(row_id < col_id, 1.0, 0.0).astype(BF16)
+
+    def slots(block, stream, expert):
+        expert = expert.astype(F32)
+        hit0 = jnp.where(block[2 * stream : 2 * stream + 1] == expert, 1.0, 0.0)
+        hit1 = jnp.where(block[2 * stream + 1 : 2 * stream + 2] == expert, 1.0, 0.0)
+        hit = hit0 + hit1
+        wide = jnp.broadcast_to(hit, (16, TOK)).astype(BF16)
+        slot = jnp.dot(wide, before, preferred_element_type=F32)[0:1]
+        gate = (
+            block[4 + 2 * stream : 5 + 2 * stream] * hit0
+            + block[5 + 2 * stream : 6 + 2 * stream] * hit1
+        )
+        return hit0, hit1, hit, slot, gate
+
+    loads[4].wait()
+    pre_copies = {}
+    for dx in range(2):
+        for i in range(2):
+            owner = z if i == 0 else 3 - z
+            expert = 2 * ((xh + dx) % 2) + owner // 2
+            hit0, hit1, _, slot, _ = slots(own_meta, 1, expert)
+            hit_row = jnp.concatenate([hit0, hit1], axis=1)
+            slot_row = jnp.concatenate([slot, slot], axis=1)
+            line = lax.broadcasted_iota(jnp.int32, (80, 2 * TOK), 0).astype(F32)
+            pick_pre[...] = jnp.where((line == slot_row) & (hit_row > 0.5), 1.0, 0.0).astype(BF16)
+            target = pre_got.at[i, xh] if (dx, i) == (0, 0) else pre_out.at[2 * dx + i]
+
+            def gather_pre(t, carry, target=target):
+                cols = pl.ds(pl.multiple_of(t * 512, 512), 512)
+                target[:, cols] = jnp.dot(
+                    pick_pre[...], pre_in[:, cols], preferred_element_type=F32
+                ).astype(BF16)
+                return carry
+
+            lax.fori_loop(0, 4, gather_pre, 0)
+            if (dx, i) != (0, 0):
+                copy = remote(
+                    pre_out.at[2 * dx + i],
+                    pre_got.at[i, xh],
+                    pre_send.at[i, dx],
+                    pre_recv.at[i, dx],
+                    place(p, dx, i * mirror, 0),
+                )
+                copy.start()
+                pre_copies[dx, i] = copy
 
     total = jnp.zeros((TOK, 1), F32)
     for q in range(4):
@@ -243,25 +300,7 @@
         copy.start()
 
     meta_copy.wait_recv()
-    own_meta = meta[...]
     got_meta = meta_got[...]
-    row_id = lax.broadcasted_iota(jnp.int32, (TOK, TOK), 0)
-    col_id = lax.broadcasted_iota(jnp.int32, (TOK, TOK), 1)
-    before = jnp.where(row_id < col_id, 1.0, 0.0).astype(BF16)
-
-    def slots(block, stream, expert):
-        expert = expert.astype(F32)
-        hit0 = jnp.where(block[2 * stream : 2 * stream + 1] == expert, 1.0, 0.0)
-        hit1 = jnp.where(block[2 * stream + 1 : 2 * stream + 2] == expert, 1.0, 0.0)
-        hit = hit0 + hit1
-        wide = jnp.broadcast_to(hit, (16, TOK)).astype(BF16)
-        slot = jnp.dot(wide, before, preferred_element_type=F32)[0:1]
-        gate = (
-            block[4 + 2 * stream : 5 + 2 * stream] * hit0
-            + block[5 + 2 * stream : 6 + 2 * stream] * hit1
-        )
-        return hit0, hit1, hit, slot, gate
-
     for stream, pick, comb in ((0, pick_f, comb_f), (1, pick_b, comb_b)):
         rows_needed = []
         for local in range(2):
@@ -294,37 +333,6 @@
             comb[pl.ds(2 * side * TOK, TOK), :] = high
             comb[pl.ds((2 * side + 1) * TOK, TOK), :] = (mix - high.astype(F32)).astype(BF16)
 
-    loads[4].wait()
-    pre_copies = {}
-    for dx in range(2):
-        for i in range(2):
-            expert = 2 * ((xh + dx) % 2) + ((z + 2 * i) % 4) // 2
-            hit0, hit1, _, slot, _ = slots(own_meta, 1, expert)
-            hit_row = jnp.concatenate([hit0, hit1], axis=1)
-            slot_row = jnp.concatenate([slot, slot], axis=1)
-            line = lax.broadcasted_iota(jnp.int32, (80, 2 * TOK), 0).astype(F32)
-            pick_pre[...] = jnp.where((line == slot_row) & (hit_row > 0.5), 1.0, 0.0).astype(BF16)
-            target = pre_got.at[i, xh] if (dx, i) == (0, 0) else pre_out.at[2 * dx + i]
-
-            def gather_pre(t, carry, target=target):
-                cols = pl.ds(pl.multiple_of(t * 512, 512), 512)
-                target[:, cols] = jnp.dot(
-                    pick_pre[...], pre_in[:, cols], preferred_element_type=F32
-                ).astype(BF16)
-                return carry
-
-            lax.fori_loop(0, 4, gather_pre, 0)
-            if (dx, i) != (0, 0):
-                copy = remote(
-                    pre_out.at[2 * dx + i],
-                    pre_got.at[i, xh],
-                    pre_send.at[i, dx],
-                    pre_recv.at[i, dx],
-                    place(p, dx, 2 * i, 0),
-                )
-                copy.start()
-                pre_copies[dx, i] = copy
-
     rows0, rows1 = pl.ds(0, ROWS), pl.ds(ROWS, ROWS)
     partner = {"pp": p, "ep": xh * 8 + (z + 1 - 2 * zp) * 2 + c}
     fwd = dict(
@@ -335,13 +343,10 @@
     )
     fwd.update(number=0, width=2 * FF)
     bwd.update(number=1, width=FF)
-    for stream in (fwd, bwd):
-        for name in ("sent", "core", "chip", "ag", "ac", "back", "over"):
-            stream[name] = {}
-
-    def dispatch(stream, dzp, dc):
+    def dispatch(stream, dzp, dc, k):
         number, v, s, x = stream["number"], stream["v"], stream["s"], stream["x"]
-        base = columns(dzp, dc)
+        begin, size = HALVES[k]
+        base = columns(dzp, dc) + begin
         targets = []
         for dz in (dzp, dzp + 2):
             here = x if (dz, dc) == (0, 0) else s
@@ -352,27 +357,17 @@
             block = v[:, cols]
             if number == 0:
                 block = (block.astype(F32) * inv_got[:, 0:1] * gain[:, cols]).astype(BF16)
-            where = pl.ds(pl.multiple_of(t * TILE, TILE), TILE)
+            where = pl.ds(pl.multiple_of(begin + t * TILE, TILE), TILE)
             for ref, dz, local in targets:
                 ref[dz, pl.ds(dc * ROWS, ROWS), where] = jnp.dot(
                     stream["pick"][local], block, preferred_element_type=F32
                 ).astype(BF16)
             return carry
 
-        lax.fori_loop(0, SLICE // TILE, gather, 0)
+        lax.fori_loop(0, size // TILE, gather, 0)
         for dz in (dzp + 2, dzp):
-            if (dz, dc) == (0, 0):
-                continue
-            rows = pl.ds(dc * ROWS, ROWS)
-            copy = remote(
-                s.at[dz, rows],
-                x.at[dz, rows],
-                d_send.at[number, dz, dc],
-                d_recv.at[number, dz, dc],
-                place(p, 0, dz, dc),
-            )
-            copy.start()
-            stream["sent"][dz, dc] = copy
+            if (dz, dc) != (0, 0):
+                moved(stream, dz, dc, k).start()
 
     def multiply(lhs, w, out, count, tile, turned):
         def step(t, carry):
@@ -388,29 +383,63 @@
 
         lax.fori_loop(0, count // tile, step, 0)
 
-    def first_product(stream, dz):
+    def moved(stream, dz, dc, k):
+        rows, cols = pl.ds(dc * ROWS, ROWS), pl.ds(*HALVES[k])
+        number = stream["number"]
+        return remote(
+            stream["s"].at[dz, rows, cols],
+            stream["x"].at[dz, rows, cols],
+            d_send.at[number, dz, dc, k],
+            d_recv.at[number, dz, dc, k],
+            place(p, 0, dz, dc),
+        )
+
+    def to_other_core(stream, dz):
+        number, width = stream["number"], stream["width"]
+        return remote(
+            part.at[dz, rows1, pl.ds(0, width)],
+            stream["r1"].at[dz],
+            r1_send.at[number, dz],
+            r1_recv.at[number, dz],
+            place(p, 0, 0, 1),
+        )
+
+    def first_product(stream, slot):
         number, x, width = stream["number"], stream["x"], stream["width"]
+        dz = slot_dz[slot]
         for dc in range(2):
-            if (dz, dc) != (0, 0):
-                stream["sent"][dz, dc].wait_recv()
+            if (slot, dc) != ("own", 0):
+                for k in range(2):
+                    moved(stream, dz, dc, k).wait_recv()
+        if number == 1:
+            to_other_core(fwd, dz).wait_send()
+            if slot in passed_on:
+                to_partner(fwd, slot).wait_send()
         out = part.at[dz, :, pl.ds(0, width)]
         if number == 0:
             multiply(x.at[dz], w1, out, width, 512, False)
         else:
             multiply(x.at[dz], w2, out, width, 512, True)
-        copy = remote(
-            part.at[dz, rows1, pl.ds(0, width)],
-            stream["r1"].at[dz],
-            r1_send.at[number, dz],
-            r1_recv.at[number, dz],
-            place(p, 0, 0, 1),
-        )
-        copy.start()
-        stream["core"][dz] = copy
-
-    def chip_sum(stream, dz):
-        number, r1, width = stream["number"], stream["r1"], stream["width"]
-        stream["core"][dz].wait_recv()
+        to_other_core(stream, dz).start()
+
+    slot_dz = {"own": 0, "near": near_z, "two": 2, "far": far_z}
+    passed_on = {"far": 0, "two": 1}
+
+    def to_partner(stream, slot):
+        number, width = stream["number"], stream["width"]
+        i = passed_on[slot]
+        return remote(
+            part.at[slot_dz[slot], rows0, pl.ds(0, width)],
+            stream["r2"].at[i],
+            r2_send.at[number, i],
+            r2_recv.at[number, i],
+            partner,
+        )
+
+    def chip_sum(stream, slot):
+        r1, width = stream["r1"], stream["width"]
+        dz = slot_dz[slot]
+        to_other_core(stream, dz).wait_recv()
 
         def add(t, carry):
             cols = pl.ds(pl.multiple_of(t * 512, 512), 512)
@@ -420,40 +449,35 @@
             return carry
 
         lax.fori_loop(0, width // 512, add, 0)
-        if dz % 2 == 1:
-            index = ((dz + 5 - 2 * zp) % 4) // 2
-            copy = remote(
-                part.at[dz, rows0, pl.ds(0, width)],
-                stream["r2"].at[index],
-                r2_send.at[number, dz // 2],
-                r2_recv.at[number, index],
-                partner,
-            )
-            copy.start()
-            stream["chip"][dz] = copy
-
-    def to_core(stream, dz):
-        number, h = stream["number"], stream["h"]
-        copy = remote(
+        if slot in passed_on:
+            to_partner(stream, slot).start()
+
+    def share_core(stream, slot):
+        number, h, dz = stream["number"], stream["h"], slot_dz[slot]
+        return remote(
             h.at[dz, rows0],
             h.at[dz, rows1],
             ac_send.at[number, dz],
             ac_recv.at[number, dz],
             place(p, 0, 0, 1),
         )
-        copy.start()
-        stream["ac"][dz] = copy
-
-    def activate(stream, dz):
-        number, h, r2, width = stream["number"], stream["h"], stream["r2"], stream["width"]
-        i = dz // 2
-        remote(
-            part.at[0, rows0, pl.ds(0, width)],
-            r2.at[i],
-            r2_send.at[number, 0],
-            r2_recv.at[number, i],
+
+    def share_partner(stream, i):
+        number, h = stream["number"], stream["h"]
+        there = 3 - 2 * (1 - zp) if i == 0 else 2
+        return remote(
+            h.at[0 if i == 0 else near_z, rows0],
+            h.at[there, rows0],
+            ag_send.at[number, i],
+            ag_recv.at[number, i],
             partner,
-        ).wait_recv()
+        )
+
+    def activate(stream, slot):
+        number, h, r2 = stream["number"], stream["h"], stream["r2"]
+        i = 0 if slot == "own" else 1
+        dz = slot_dz[slot]
+        to_partner(stream, "far" if i == 0 else "two").wait_recv()
         if number == 1:
             for dx in range(2):
                 if (dx, i) != (0, 0):
@@ -480,113 +504,113 @@
             return carry
 
         lax.fori_loop(0, FF // TILE, step, 0)
-        there = (dz + 5 - 2 * zp) % 4
-        copy = remote(
-            h.at[dz, rows0],
-            h.at[there, rows0],
-            ag_send.at[number, i],
-            ag_recv.at[number, there // 2],
-            partner,
-        )
-        copy.start()
-        stream["ag"][dz] = copy
-        to_core(stream, dz)
-
-    def forward_on(stream, dz):
-        number, h = stream["number"], stream["h"]
-        i = dz // 2
-        remote(
-            h.at[dz - 1, rows0],
-            h.at[dz, rows0],
-            ag_send.at[number, i],
-            ag_recv.at[number, i],
-            partner,
-        ).wait_recv()
-        to_core(stream, dz)
-
-    def second_product(stream, dz):
-        number, h, s, ret = stream["number"], stream["h"], stream["s"], stream["ret"]
-        region = ret.at[
-            pl.ds(pl.multiple_of(z // 2 * ROWS, ROWS), ROWS), pl.ds(columns(0, 0), SLICE)
+        share_partner(stream, i).start()
+        share_core(stream, slot).start()
+
+    def forward_on(stream, slot):
+        share_partner(stream, passed_on[slot]).wait_recv()
+        share_core(stream, slot).start()
+
+    def back(stream, dz, dc, n):
+        number, s = stream["number"], stream["s"]
+        begin, size = PIECES[n]
+        region = stream["ret"].at[
+            pl.ds(pl.multiple_of(z // 2 * ROWS, ROWS), ROWS),
+            pl.ds(pl.multiple_of(columns(0, 0) + begin, TILE), size),
         ]
-        stream["ac"][dz].wait_recv()
-        for dc in range(2):
-            if (dz, dc) != (0, 0):
-                stream["sent"][dz, dc].wait_send()
+        source = s.at[dz, pl.ds(dc * ROWS, ROWS), pl.ds(begin, size)]
+        if isinstance(dz, int) and (dz, dc) == (0, 0):
+            return pltpu.make_async_copy(source, region, ret_recv.at[number, 0, 0, n])
+        return remote(
+            source,
+            region,
+            ret_send.at[number, dz, dc, n],
+            ret_recv.at[number, dz, dc, n],
+            place(p, 0, 4 - dz, dc),
+        )
+
+    def second_product(stream, slot, n):
+        number, h, s = stream["number"], stream["h"], stream["s"]
+        dz = slot_dz[slot]
+        begin, size = PIECES[n]
+        if n == 0:
+            share_core(stream, slot).wait_recv()
+            for dc in range(2):
+                if (slot, dc) != ("own", 0):
+                    for k in range(2):
+                        moved(stream, dz, dc, k).wait_send()
+        out = s.at[dz, :, pl.ds(begin, size)]
         if number == 0:
-            multiply(h.at[dz], w2, s.at[dz], SLICE, TILE, False)
+            multiply(h.at[dz], w2.at[:, pl.ds(begin, size)], out, size, TILE, False)
         else:
-            multiply(h.at[dz], w1, s.at[dz], SLICE, TILE, True)
-        for dc in range(2):
-            rows = pl.ds(dc * ROWS, ROWS)
-            if (dz, dc) == (0, 0):
-                copy = pltpu.make_async_copy(s.at[dz, rows], region, ret_recv.at[number, 0, 0])
-            else:
-                copy = remote(
-                    s.at[dz, rows],
-                    region,
-                    ret_send.at[number, dz, dc],
-                    ret_recv.at[number, dz, dc],
-                    place(p, 0, 4 - dz, dc),
-                )
-            copy.start()
-            stream["back"][dz, dc] = copy
-
-    def combine(stream, dzp):
-        number, v, x, ret = stream["number"], stream["v"], stream["x"], stream["ret"]
+            multiply(h.at[dz], w1.at[pl.ds(begin, size)], out, size, TILE, True)
+        for dc in (1, 0):
+            back(stream, dz, dc, n).start()
+
+    def cross(stream, dzp, dc, n):
+        number, v = stream["number"], stream["v"]
+        begin, size = PIECES[n]
+        cols = pl.ds(pl.multiple_of(columns(dzp, dc) + begin, TILE), size)
+        return remote(
+            v.at[pl.ds(other_row, TOK), cols],
+            stream["xr"].at[:, cols],
+            x_send.at[number, n, 2 * dzp + dc],
+            x_recv.at[number, n, 2 * dzp + dc],
+            place(p, 1, 0, 0),
+        )
+
+    def combine(stream, n):
+        v, x, ret = stream["v"], stream["x"], stream["ret"]
+        begin, size = PIECES[n]
         fetches = []
-        for dc in (1, 0):
+        for dzp, dc in late:
             for dz in (dzp, dzp + 2):
                 if (dz, dc) == (0, 0):
-                    stream["back"][dz, dc].wait()
+                    back(stream, dz, dc, n).wait()
                 else:
-                    stream["back"][dz, dc].wait_recv()
+                    back(stream, dz, dc, n).wait_recv()
+            jr = 2 * dzp + dc
+            cols = pl.ds(pl.multiple_of(columns(dzp, dc) + begin, TILE), size)
             fetch = pltpu.make_async_copy(
-                ret.at[:, pl.ds(columns(dzp, dc), SLICE)], stage.at[dc], stage_sem.at[dc]
+                ret.at[:, cols], stage.at[jr, :, pl.ds(0, size)], stage_sem.at[jr]
             )
             fetch.start()
             fetches.append(fetch)
-        for dc in (1, 0):
-            fetches[1 - dc].wait()
-            base = columns(dzp, dc)
+        for fetch, (dzp, dc) in zip(fetches, late):
+            fetch.wait()
+            base = columns(dzp, dc) + begin
             jr = 2 * dzp + dc
 
-            def step(t, carry, dc=dc, base=base, jr=jr):
+            def step(t, carry, base=base, jr=jr):
                 cols = pl.ds(pl.multiple_of(t * TILE, TILE), TILE)
                 mixed = jnp.dot(
-                    stream["comb"][...], stage[dc, :, cols], preferred_element_type=F32
+                    stream["comb"][...], stage[jr, :, cols], preferred_element_type=F32
                 )
                 own = mixed[0:TOK] + mixed[TOK : 2 * TOK]
                 other = mixed[2 * TOK : 3 * TOK] + mixed[3 * TOK :]
                 high = own.astype(BF16)
-                x[jr, pl.ds(0, TOK), cols] = high
-                x[jr, pl.ds(TOK, TOK), cols] = (own - high.astype(F32)).astype(BF16)
+                kept = pl.ds(pl.multiple_of(begin + t * TILE, TILE), TILE)
+                x[jr, pl.ds(0, TOK), kept] = high
+                x[jr, pl.ds(TOK, TOK), kept] = (own - high.astype(F32)).astype(BF16)
                 out_cols = pl.ds(pl.multiple_of(base + t * TILE, TILE), TILE)
                 v[pl.ds(other_row, TOK), out_cols] = other.astype(BF16)
                 return carry
 
-            lax.fori_loop(0, SLICE // TILE, step, 0)
-            copy = remote(
-                v.at[pl.ds(other_row, TOK), pl.ds(base, SLICE)],
-                stream["xr"].at[:, pl.ds(base, SLICE)],
-                x_send.at[number, jr],
-                x_recv.at[number, jr],
-                place(p, 1, 0, 0),
-            )
-            copy.start()
-            stream["over"][dzp, dc] = copy
+            lax.fori_loop(0, size // TILE, step, 0)
+            cross(stream, dzp, dc, n).start()
 
     late = [(0, 1), (0, 0), (1, 1), (1, 0)]
 
-    def finish_forward(crossed):
+    def finish_forward(n):
+        begin, size = PIECES[n]
         for dzp, dc in late:
-            crossed[dzp, dc].wait_recv()
+            cross(fwd, dzp, dc, n).wait_recv()
             base = columns(dzp, dc)
             jr = 2 * dzp + dc
 
             def step(t, carry, base=base, jr=jr):
-                cols = pl.ds(pl.multiple_of(t * TILE, TILE), TILE)
-                wide = pl.ds(pl.multiple_of(base + t * TILE, TILE), TILE)
+                cols = pl.ds(pl.multiple_of(begin + t * TILE, TILE), TILE)
+                wide = pl.ds(pl.multiple_of(base + begin + t * TILE, TILE), TILE)
                 here = pl.ds(own_row, TOK)
                 mine = x_f[jr, pl.ds(0, TOK), cols].astype(F32)
                 mine = mine + x_f[jr, pl.ds(TOK, TOK), cols].astype(F32)
@@ -595,31 +619,31 @@
                 ).astype(BF16)
                 return carry
 
-            lax.fori_loop(0, SLICE // TILE, step, 0)
-            copy = pltpu.make_async_copy(
-                v_f.at[pl.ds(own_row, TOK), pl.ds(base, SLICE)],
-                fwd_out.at[:, pl.ds(base, SLICE)],
-                out_sem.at[0, jr],
-            )
-            copy.start()
-            outs.append(copy)
-
-    def finish_backward(crossed):
+            lax.fori_loop(0, size // TILE, step, 0)
+
+    def write_forward():
+        copy = pltpu.make_async_copy(v_f.at[pl.ds(own_row, TOK)], fwd_out, out_sem.at[0, 0])
+        copy.start()
+        outs.append(copy)
+
+    def backward_start():
         total = jnp.zeros((TOK, 1), F32)
         for n, (dzp, dc) in enumerate(late):
             saved_loads[n].wait()
             block = s_f[2 * dzp + dc, pl.ds(0, TOK), :].astype(F32)
             total = total + jnp.sum(block * block, axis=1, keepdims=True)
-        inv = lax.rsqrt(total / D + EPS)
-        dots = jnp.zeros((TOK, TILE), F32)
+        return lax.rsqrt(total / D + EPS)
+
+    def backward_piece(n, inv, dots):
+        begin, size = PIECES[n]
         for dzp, dc in late:
-            crossed[dzp, dc].wait_recv()
+            cross(bwd, dzp, dc, n).wait_recv()
             base = columns(dzp, dc)
             jr = 2 * dzp + dc
 
             def step(t, carry, base=base, jr=jr):
-                cols = pl.ds(pl.multiple_of(t * TILE, TILE), TILE)
-                wide = pl.ds(pl.multiple_of(base + t * TILE, TILE), TILE)
+                cols = pl.ds(pl.multiple_of(begin + t * TILE, TILE), TILE)
+                wide = pl.ds(pl.multiple_of(base + begin + t * TILE, TILE), TILE)
                 grad = x_b[jr, pl.ds(0, TOK), cols].astype(F32)
                 grad = grad + x_b[jr, pl.ds(TOK, TOK), cols].astype(F32)
                 grad = grad + xr_b[:, wide].astype(F32)
@@ -630,7 +654,10 @@
                 local_gain[:, wide] = jnp.sum(grad * w * inv, axis=0, keepdims=True)
                 return carry + w * gain[:, wide] * grad
 
-            dots = lax.fori_loop(0, SLICE // TILE, step, dots)
+            dots = lax.fori_loop(0, size // TILE, step, dots)
+        return dots
+
+    def finish_backward(inv, dots):
         scale = inv * inv * inv * (jnp.sum(dots, axis=1, keepdims=True) / D)
         waiting = gain_cores()
         for n, (dzp, dc) in enumerate(late):
@@ -729,71 +756,84 @@
         copy.wait_recv()
 
     def dispatch_forward(n):
-        relay_forward(pairs[n])
-        arrived(0, v_f, pairs[n])
-        if n + 2 < 4:
-            start_forward(pairs[n + 2])
-        else:
-            relay_backward(pairs[n - 2])
-        dispatch(fwd, *pairs[n])
+        for i in (2 * n, 2 * n + 1):
+            relay_forward(pairs[i])
+            start_backward(pairs[i])
+            arrived(0, v_f, pairs[i])
+            if i < 6:
+                start_forward(pairs[i + 2])
+            dispatch(fwd, *pairs[i])
 
     def dispatch_backward(n):
-        arrived(1, v_b, pairs[n])
-        dispatch(bwd, *pairs[n])
-
-    def first_product_again(dz):
-        fwd["core"][dz].wait_send()
-        if dz % 2 == 1:
-            fwd["chip"][dz].wait_send()
-        first_product(bwd, dz)
+        for i in (2 * n, 2 * n + 1):
+            arrived(1, v_b, pairs[i])
+            if i + 3 < 8:
+                relay_backward(pairs[i + 3])
+            dispatch(bwd, *pairs[i])
 
     dispatch_forward(0)
     dispatch_forward(1)
     dispatch_forward(2)
     loads[5].wait()
-    first_product(fwd, 1)
-    first_product(fwd, 3)
+    first_product(fwd, "two")
     dispatch_forward(3)
-    chip_sum(fwd, 1)
-    chip_sum(fwd, 3)
-    relay_backward(pairs[2])
-    relay_backward(pairs[3])
-    first_product(fwd, 0)
-    first_product(fwd, 2)
-    chip_sum(fwd, 0)
-    chip_sum(fwd, 2)
+    chip_sum(fwd, "two")
+    for pair in pairs[:3]:
+        relay_backward(pair)
+    first_product(fwd, "far")
+    first_product(fwd, "own")
+    chip_sum(fwd, "far")
+    first_product(fwd, "near")
+    chip_sum(fwd, "own")
+    chip_sum(fwd, "near")
     loads[6].wait()
     dispatch_backward(0)
     dispatch_backward(1)
-    activate(fwd, 0)
-    activate(fwd, 2)
+    activate(fwd, "near")
+    activate(fwd, "own")
     dispatch_backward(2)
-    second_product(fwd, 0)
-    second_product(fwd, 2)
-    first_product_again(1)
-    first_product_again(3)
-    forward_on(fwd, 1)
-    forward_on(fwd, 3)
     dispatch_backward(3)
-    second_product(fwd, 1)
-    second_product(fwd, 3)
-    chip_sum(bwd, 1)
-    chip_sum(bwd, 3)
-    first_product_again(0)
-    first_product_again(2)
-    chip_sum(bwd, 0)
-    chip_sum(bwd, 2)
+    for n in (0, 1):
+        second_product(fwd, "own", n)
+        second_product(fwd, "near", n)
+    first_product(bwd, "two")
+    chip_sum(bwd, "two")
+    forward_on(fwd, "two")
+    forward_on(fwd, "far")
+    for n in (0, 1):
+        second_product(fwd, "two", n)
+        second_product(fwd, "far", n)
+    first_product(bwd, "far")
+    chip_sum(bwd, "far")
+    for n in (2, 3):
+        for slot in ("two", "far", "own", "near"):
+            second_product(fwd, slot, n)
+    first_product(bwd, "own")
+    first_product(bwd, "near")
+    chip_sum(bwd, "own")
+    chip_sum(bwd, "near")
     combine(fwd, 0)
-    activate(bwd, 0)
-    activate(bwd, 2)
+    activate(bwd, "near")
+    activate(bwd, "own")
     combine(fwd, 1)
-    second_product(bwd, 0)
-    second_product(bwd, 2)
-    forward_on(bwd, 1)
-    forward_on(bwd, 3)
-    second_product(bwd, 1)
-    second_product(bwd, 3)
-    sends_done([copy for key, copy in fwd["back"].items() if key != (0, 0)])
+    for n in (0, 1):
+        second_product(bwd, "own", n)
+        second_product(bwd, "near", n)
+    combine(fwd, 2)
+    combine(fwd, 3)
+    forward_on(bwd, "two")
+    forward_on(bwd, "far")
+    for n in (0, 1):
+        second_product(bwd, "two", n)
+        second_product(bwd, "far", n)
+    for n in (2, 3):
+        for slot in ("two", "far", "own", "near"):
+            second_product(bwd, slot, n)
+    for n in range(4):
+        for dz in range(4):
+            for dc in range(2):
+                if (dz, dc) != (0, 0):
+                    back(fwd, dz, dc, n).wait_send()
     saved_loads = []
     for n, (dzp, dc) in enumerate(late):
         copy = pltpu.make_async_copy(
@@ -803,10 +843,20 @@
         )
         copy.start()
         saved_loads.append(copy)
+    for n in range(4):
+        finish_forward(n)
+    write_forward()
+    inv = backward_start()
+    dots = jnp.zeros((TOK, TILE), F32)
     combine(bwd, 0)
     combine(bwd, 1)
-    finish_forward(fwd["over"])
-    finish_backward(bwd["over"])
+    dots = backward_piece(0, inv, dots)
+    combine(bwd, 2)
+    dots = backward_piece(1, inv, dots)
+    combine(bwd, 3)
+    dots = backward_piece(2, inv, dots)
+    dots = backward_piece(3, inv, dots)
+    finish_backward(inv, dots)
 
     sends_done([meta_copy] + inv_copies + list(pre_copies.values()) + gain_copies)
     for pair in pairs:
@@ -816,11 +866,22 @@
         for copy in block_copies(relay, v_f, far_send, s1_recv, *pair, 0):
             copy.wait_send()
     for stream in (fwd, bwd):
-        for name in ("ag", "ac", "over"):
-            sends_done(stream[name].values())
-    for name in ("core", "chip"):
-        sends_done(bwd[name].values())
-    sends_done([copy for key, copy in bwd["back"].items() if key != (0, 0)])
+        for slot in slot_dz:
+            share_core(stream, slot).wait_send()
+        for i in range(2):
+            share_partner(stream, i).wait_send()
+        for n in range(4):
+            for dzp, dc in late:
+                cross(stream, dzp, dc, n).wait_send()
+    for slot in slot_dz:
+        to_other_core(bwd, slot_dz[slot]).wait_send()
+    for slot in passed_on:
+        to_partner(bwd, slot).wait_send()
+    for n in range(4):
+        for dz in range(4):
+            for dc in range(2):
+                if (dz, dc) != (0, 0):
+                    back(bwd, dz, dc, n).wait_send()
     for copy in outs:
         copy.wait()
 
@@ -888,7 +949,7 @@
             buf(2 * TOK, 2 * FF),
             buf(4, 80, 2 * FF),
             buf(2, 2, 80, 2 * FF),
-            buf(2, 2 * ROWS, SLICE),
+            buf(4, 2 * ROWS, 512),
             pltpu.VMEM((8, TOK), F32),
             pltpu.VMEM((TOK, 128), F32),
             pltpu.VMEM((2 * TOK, 128), F32),
@@ -898,24 +959,24 @@
             buf(4 * TOK, 2 * ROWS),
             buf(4 * TOK, 2 * ROWS),
             dma((8,)),
-            dma((2,)),
+            dma((4,)),
             dma((2, 4)),
             dma((4,)),
             dma((4,)),
             dma((2, 2)),
             dma((2, 2)),
             buf(TOK, D),
-            dma((4, 2)),
-            dma((4, 2)),
-            dma((4,)),
-            dma((4,)),
-            dma((2, 4, 2)),
+            dma((8, 2)),
+            dma((8, 2)),
+            dma((8,)),
+            dma((8,)),
+            dma((2, 8, 2)),
             pltpu.VMEM((1, D), F32),
             pltpu.VMEM((8, PART), F32),
             dma((16,)),
             dma((16,)),
-            dma((2, 4, 2)),
-            dma((2, 4, 2)),
+            dma((2, 4, 2, 2)),
+            dma((2, 4, 2, 2)),
             dma((2, 4)),
             dma((2, 4)),
             dma((2, 2)),
@@ -924,10 +985,10 @@
             dma((2, 2)),
             dma((2, 4)),
             dma((2, 4)),
-            dma((2, 4, 2)),
-            dma((2, 4, 2)),
-            dma((2, 4)),
-            dma((2, 4)),
+            dma((2, 4, 2, 4)),
+            dma((2, 4, 2, 4)),
+            dma((2, 4, 4)),
+            dma((2, 4, 4)),
         ],
         compiler_params=pltpu.CompilerParams(
             collective_id=0, has_side_effects=True, vmem_limit_bytes=64 * 2**20 - 2**16

time: 372 us -> 340 us (0.914)
  Pallas kernels: 359 us -> 327 us
    pallas_call x1, Pallas kernels: 359 us -> 327 us  [on_device(): pl.pallas_call(kernel, out_shape=(jax.ShapeDtypeStruct((TOK, D), BF16), j...]
where the time goes in v3:
time: 340 us; the launch traced here: 337 us
  Pallas kernels  327 us (96%)
  local copies, waits for them, and re-layouts  7.37 us (2%)
    pallas_call x1, Pallas kernels, on_device(): pl.pallas_call(kernel, out_shape=(jax.ShapeDtypeStruct((TOK, D), BF16), j...  327 us

profile of v3, /device:TPU:16, one launch (start us, length us, event | category | flops | bytes accessed | tf_op | source)
XLA Modules:
  0.0 336.7 jit_solution(5347485113132810924)
XLA Ops:
  0.6 0.7 convert_bitcast_fusion
  1.3 1.3 pad_maximum_fusion.meta
  2.6 2.5 copy.14
  5.2 326.7 %experts.1 = (bf16[128,7168]{1,0:T(8,128)(2,1)}, bf16[128,7168]{1,0:T(8,128)(2,1)}, f32[1,7168]{1,0:T(1,128)}, bf16[288,7168]{1,0:T(8,128)(2,1)}, bf16[288,7168]{1,0:T(8,128)(2,1)}) custom-call(f32[8,128]{1,0:T(8,128)} %pad_maximum_fusion.meta, f32[1,7168]{1,0:T(1,128)} %gain.1, bf16[128,7168]{1,0:T(8,128)(2,1)} %bitcast.33, bf16[128,7168]{1,0:T(8,128)(2,1)} %bitcast.34, ...), custom_call_target="tpu_custom_call" | custom-call | flops 25999998976 | bytes 40000000 | tf_op jit(solution)/shard_map/experts/pallas_call | solution.py:919
  331.9 0.0 copy-start
  331.9 3.0 copy.18
  334.9 0.0 copy-done
  334.9 0.0 copy-start.1
  334.9 1.2 copy.19
  336.1 0.0 copy-done.1
  336.1 0.6 copy.20
Async XLA Ops:
  331.9 3.0 copy-start
  334.9 1.2 copy-start.1
